TPU v7x, 128 devices: a whole 4x4x4 slice. The times are simulated.
128 devices in a mesh: pipe: 2 (over core), fsdp: 16 (over z, y), tp: 4 (over x).
Axes of the slice: x: 4, y: 4, z: 4, core: 2. Of those that a mesh axis runs over, the one named last changes fastest.
Arguments:
- boundary: bfloat16 [2, 2, 12608, 768], P('pipe', None, ('fsdp', 'tp')), may hold values from -6 to 6
- loads: int32 [2, 16], P(None, 'fsdp'), may hold values from 1 to 4, as said below
- norm_gains: bfloat16 [2, 2, 768], P('pipe', None, ('fsdp', 'tp')), may hold values from 0.5 to 1.5
- row_biases: bfloat16 [2, 4, 768], P('pipe', None, ('fsdp', 'tp')), may hold values from -1.796875 to 1.796875
- w_qkv: bfloat16 [2, 768, 3, 12, 64], P('pipe', 'fsdp', None, 'tp'), may hold values from -0.21875 to 0.21875
- qv_bias: bfloat16 [2, 2, 12, 64], P('pipe', None, 'tp', 'fsdp'), may hold values from -1.796875 to 1.796875
- w_out: bfloat16 [2, 12, 64, 768], P('pipe', 'tp', None, 'fsdp'), may hold values from -0.875 to 0.875
- w_up: bfloat16 [2, 768, 3072], P('pipe', None, ('fsdp', 'tp')), may hold values from -0.21875 to 0.21875
- up_bias: bfloat16 [2, 3072], P('pipe', ('fsdp', 'tp')), may hold values from -1.796875 to 1.796875
- w_down: bfloat16 [2, 3072, 768], P('pipe', ('fsdp', 'tp')), may hold values from -0.109375 to 0.109375
Outputs:
- ends: bfloat16 [2, 2, 12608, 768], P('pipe', None, ('fsdp', 'tp'))
- grad_gains: float32 [2, 2, 768], P('pipe', None, ('fsdp', 'tp'))
- grad_biases: float32 [2, 4, 768], P('pipe', None, ('fsdp', 'tp'))
- grad_qkv: float32 [2, 768, 3, 12, 64], P('pipe', 'fsdp', None, 'tp')
- grad_qv_bias: float32 [2, 2, 12, 64], P('pipe', None, 'tp', 'fsdp')
- grad_out: float32 [2, 12, 64, 768], P('pipe', 'tp', None, 'fsdp')
- grad_up: float32 [2, 768, 3072], P('pipe', None, ('fsdp', 'tp'))
- grad_up_bias: float32 [2, 3072], P('pipe', ('fsdp', 'tp'))
- grad_down: float32 [2, 3072, 768], P('pipe', ('fsdp', 'tp'))
Inputs may be any that keep to these rules, and one draw needn't show every extreme that they name: loads[m, f] is the number of live images of image group f in micro-batch m; its live images are the first slots; in every micro-batch some group has all 4 slots live.
All inputs are finite; a program needn't handle non-finite values.
Results may differ from a plain program's by a relative error of at most 0.024.
Values may be sent and summed in bfloat16 or wider, within the bound.
A program may use at most 128 MiB of HBM per device.

v0:
```python
from functools import partial

import jax
import jax.numpy as jnp
from jax import lax
from jax.sharding import PartitionSpec as P

SEQ = 197


epsilon = 1e-06
inv_root2 = 0.7071067811865476
inv_root_two_pi = 0.3989422804014327


def shifted(value, axis, by):
    count = lax.axis_size(axis)
    pairs = [(i, i + by) for i in range(count) if 0 <= i + by < count]
    return lax.ppermute(value, axis, pairs)


def layer_norm(values, gain, shift):
    center = values - jnp.mean(values, -1, keepdims=True)
    spread = jnp.mean(center * center, -1, keepdims=True)
    inv_std = lax.rsqrt(spread + epsilon)
    normal = center * inv_std
    return (normal * gain + shift, normal, inv_std)


def norm_back(grad, normal, inv_std, gain):
    scaled = grad * gain
    return inv_std * (
        scaled
        - jnp.mean(scaled, -1, keepdims=True)
        - normal * jnp.mean(scaled * normal, -1, keepdims=True)
    )


def spread_rows(values):
    return lax.all_gather(values, "tp", axis=0, tiled=True)


def sum_rows(partial_sum):
    return lax.psum_scatter(
        partial_sum.astype(jnp.bfloat16), "tp", scatter_dimension=0, tiled=True
    ).astype(jnp.float32)


def spread_grads(values):
    return lax.all_gather(values, "tp", axis=0, tiled=True)


def sum_grads(partial_sum):
    return lax.psum_scatter(
        partial_sum.astype(jnp.bfloat16), "tp", scatter_dimension=0, tiled=True
    ).astype(jnp.float32)


def forward(inputs, matrices, vectors):
    in_proj, qv_bias, out_proj, up_proj, up_bias, down_proj = matrices
    gain_rows = vectors[0].astype(jnp.float32)
    bias_rows = vectors[1].astype(jnp.float32)
    norm_one, normal_one, inv_one = layer_norm(inputs, gain_rows[0], bias_rows[0])
    full_one = spread_rows(norm_one.astype(jnp.bfloat16))
    all_rows = full_one.shape[0]
    head_count = in_proj.shape[2]
    head_size = in_proj.shape[3]
    images = all_rows // SEQ
    bias_three = jnp.stack([qv_bias[0], jnp.zeros_like(qv_bias[0]), qv_bias[1]], 0).astype(
        jnp.float32
    )
    qkv = (
        jnp.einsum("rd,dthe->rthe", full_one, in_proj, preferred_element_type=jnp.float32)
        + bias_three
    ).astype(jnp.bfloat16)
    split_qkv = qkv.reshape(images, SEQ, 3, head_count, head_size)
    query_rows = split_qkv[:, :, 0]
    key_rows = split_qkv[:, :, 1]
    value_rows = split_qkv[:, :, 2]
    scale = head_size ** (-0.5)
    scores = (
        jnp.einsum("cqhe,ckhe->chqk", query_rows, key_rows, preferred_element_type=jnp.float32)
        * scale
    )
    peak_score = jnp.max(scores, -1, keepdims=True)
    expanded = jnp.exp(scores - peak_score)
    exp_total = jnp.sum(expanded, -1, keepdims=True)
    log_total = peak_score + jnp.log(exp_total)
    probs = (expanded / exp_total).astype(jnp.bfloat16)
    mixed = jnp.einsum("chqk,ckhe->cqhe", probs, value_rows, preferred_element_type=jnp.float32)
    mixed = mixed.astype(jnp.bfloat16).reshape(all_rows, head_count * head_size)
    out_flat = out_proj.reshape(head_count * head_size, out_proj.shape[2])
    attn = sum_rows(jnp.dot(mixed, out_flat, preferred_element_type=jnp.float32))
    middle = inputs + attn + bias_rows[1]
    norm_two, normal_two, inv_two = layer_norm(middle, gain_rows[1], bias_rows[2])
    full_two = spread_rows(norm_two.astype(jnp.bfloat16))
    upper = jnp.dot(full_two, up_proj, preferred_element_type=jnp.float32) + up_bias.astype(
        jnp.float32
    )
    activated = jax.nn.gelu(upper, approximate=False).astype(jnp.bfloat16)
    result = (
        middle
        + sum_rows(jnp.dot(activated, down_proj, preferred_element_type=jnp.float32))
        + bias_rows[3]
    )
    saved = (
        normal_one,
        inv_one,
        full_one,
        qkv,
        log_total,
        mixed,
        normal_two,
        inv_two,
        full_two,
        upper,
        activated,
    )
    return (result, saved)


def backward(grad, saved, matrices, vectors):
    (
        normal_one,
        inv_one,
        full_one,
        qkv,
        log_total,
        mixed,
        normal_two,
        inv_two,
        full_two,
        upper,
        activated,
    ) = saved
    in_proj, qv_bias, out_proj, up_proj, up_bias, down_proj = matrices
    gain_rows = vectors[0].astype(jnp.float32)
    grad_low = grad.astype(jnp.bfloat16)
    grad_full = spread_grads(grad_low)
    d_outbias = jnp.sum(grad_low.astype(jnp.float32), 0)
    d_down = jnp.einsum("rf,rd->fd", activated, grad_full, preferred_element_type=jnp.float32)
    d_active = jnp.einsum("rd,fd->rf", grad_full, down_proj, preferred_element_type=jnp.float32)
    normal_cdf = 0.5 * (1.0 + lax.erf(upper * inv_root2))
    density = jnp.exp(-0.5 * upper * upper) * inv_root_two_pi
    d_upper = (d_active * (normal_cdf + upper * density)).astype(jnp.bfloat16)
    d_upbias = jnp.sum(d_upper.astype(jnp.float32), 0)
    d_up = jnp.einsum("rd,rf->df", full_two, d_upper, preferred_element_type=jnp.float32)
    d_norm_two = sum_grads(
        jnp.einsum("rf,df->rd", d_upper, up_proj, preferred_element_type=jnp.float32)
    )
    d_gain_two = jnp.sum(d_norm_two * normal_two, 0)
    d_shift_two = jnp.sum(d_norm_two, 0)
    d_middle = grad + norm_back(d_norm_two, normal_two, inv_two, gain_rows[1])
    middle_low = d_middle.astype(jnp.bfloat16)
    middle_full = spread_grads(middle_low)
    d_attnbias = jnp.sum(middle_low.astype(jnp.float32), 0)
    head_count = out_proj.shape[0]
    head_size = out_proj.shape[1]
    out_flat = out_proj.reshape(head_count * head_size, out_proj.shape[2])
    d_outproj = jnp.einsum(
        "rf,rd->fd", mixed, middle_full, preferred_element_type=jnp.float32
    ).reshape(out_proj.shape)
    d_mixed = jnp.einsum(
        "rd,fd->rf", middle_full, out_flat, preferred_element_type=jnp.float32
    ).astype(jnp.bfloat16)
    all_rows = mixed.shape[0]
    images = all_rows // SEQ
    split_qkv = qkv.reshape(images, SEQ, 3, head_count, head_size)
    query_rows = split_qkv[:, :, 0]
    key_rows = split_qkv[:, :, 1]
    value_rows = split_qkv[:, :, 2]
    d_heads = d_mixed.reshape(images, SEQ, head_count, head_size)
    scale = head_size ** (-0.5)
    scores = (
        jnp.einsum("cqhe,ckhe->chqk", query_rows, key_rows, preferred_element_type=jnp.float32)
        * scale
    )
    probs = jnp.exp(scores - log_total)
    probs_low = probs.astype(jnp.bfloat16)
    d_value = jnp.einsum("chqk,cqhe->ckhe", probs_low, d_heads, preferred_element_type=jnp.float32)
    d_probs = jnp.einsum("cqhe,ckhe->chqk", d_heads, value_rows, preferred_element_type=jnp.float32)
    d_scores = (probs * (d_probs - jnp.sum(d_probs * probs, -1, keepdims=True))).astype(
        jnp.bfloat16
    )
    d_query = (
        jnp.einsum("chqk,ckhe->cqhe", d_scores, key_rows, preferred_element_type=jnp.float32)
        * scale
    )
    d_key = (
        jnp.einsum("chqk,cqhe->ckhe", d_scores, query_rows, preferred_element_type=jnp.float32)
        * scale
    )
    d_qkv = (
        jnp.stack([d_query, d_key, d_value], 2)
        .astype(jnp.bfloat16)
        .reshape(all_rows, 3, head_count, head_size)
    )
    qkv_sums = jnp.sum(d_qkv.astype(jnp.float32), 0)
    d_qvbias = jnp.stack([qkv_sums[0], qkv_sums[2]], 0)
    d_inproj = jnp.einsum("rd,rthe->dthe", full_one, d_qkv, preferred_element_type=jnp.float32)
    d_norm_one = sum_grads(
        jnp.einsum("rthe,dthe->rd", d_qkv, in_proj, preferred_element_type=jnp.float32)
    )
    d_gain_one = jnp.sum(d_norm_one * normal_one, 0)
    d_shift_one = jnp.sum(d_norm_one, 0)
    d_inputs = d_middle + norm_back(d_norm_one, normal_one, inv_one, gain_rows[0])
    matrix_grads = (d_inproj, d_qvbias, d_outproj, d_up, d_upbias, d_down)
    vector_grads = (
        jnp.stack([d_gain_one, d_gain_two], 0),
        jnp.stack([d_shift_one, d_attnbias, d_shift_two, d_outbias], 0),
    )
    return (d_inputs, matrix_grads, vector_grads)


def add_trees(left, right):
    if left is None:
        return right
    return jax.tree.map(jnp.add, left, right)


def on_device(
    boundary, loads, norm_gains, row_biases, w_qkv, qv_bias, w_out, w_up, up_bias, w_down
):
    first_section = lax.axis_index("pipe") == 0
    local_rows = boundary[0]
    batches = local_rows.shape[0]
    row_count = local_rows.shape[1]
    model_width = local_rows.shape[2]
    tp_index = lax.axis_index("tp")
    image_of = (tp_index * row_count + jnp.arange(row_count, dtype=jnp.int32)) // SEQ

    def live_rows(batch):
        return (image_of < loads[batch, 0]).astype(jnp.float32)[:, None]

    shards = (w_qkv[0], qv_bias[0], w_out[0], w_up[0], up_bias[0], w_down[0])
    vector_shards = (norm_gains[0], row_biases[0])

    def fetch():
        matrices = (
            lax.all_gather(shards[0], "fsdp", axis=0, tiled=True),
            lax.all_gather(shards[1], "fsdp", axis=2, tiled=True),
            lax.all_gather(shards[2], "fsdp", axis=2, tiled=True),
            lax.all_gather(shards[3], "fsdp", axis=1, tiled=True),
            lax.all_gather(shards[4], "fsdp", axis=0, tiled=True),
            lax.all_gather(shards[5], "fsdp", axis=0, tiled=True),
        )
        vectors = (
            lax.all_gather(vector_shards[0], ("fsdp", "tp"), axis=1, tiled=True),
            lax.all_gather(vector_shards[1], ("fsdp", "tp"), axis=1, tiled=True),
        )
        return (matrices, vectors)

    def current():
        return fetch()

    zero_rows = jnp.zeros((row_count, model_width), jnp.float32)
    stash = {}
    outputs_fwd = {}
    outputs_back = {}
    sent_up = zero_rows
    sent_down = zero_rows
    totals = None
    for clock in range(batches + 2):
        if clock <= batches:
            matrices, vectors = current()
            if clock < batches:
                own_input = local_rows[clock].astype(jnp.float32)
            else:
                own_input = zero_rows
            inputs = jnp.where(first_section, own_input, sent_up)
            result, saved = forward(inputs, matrices, vectors)
            stash[clock] = saved
            if clock >= 1:
                outputs_fwd[clock - 1] = (result * live_rows(clock - 1)).astype(jnp.bfloat16)
            if clock < batches:
                sent_up = shifted(result.astype(jnp.bfloat16), "pipe", 1).astype(jnp.float32)
        if clock >= 1:
            matrices, vectors = current()
            front = stash[clock - 2] if clock >= 2 else stash[clock]
            behind = stash[clock] if clock <= batches else stash[clock - 2]
            saved = jax.tree.map(partial(jnp.where, first_section), front, behind)
            if clock <= batches:
                last_grad = local_rows[clock - 1].astype(jnp.float32) * live_rows(clock - 1)
            else:
                last_grad = zero_rows
            grad = jnp.where(first_section, sent_down, last_grad)
            d_inputs, matrix_grads, vector_grads = backward(grad, saved, matrices, vectors)
            if clock >= 2:
                outputs_back[clock - 2] = d_inputs.astype(jnp.bfloat16)
            if clock <= batches:
                sent_down = shifted(d_inputs.astype(jnp.bfloat16), "pipe", -1).astype(jnp.float32)
            matrix_part = (
                lax.psum_scatter(
                    matrix_grads[0].astype(jnp.bfloat16), "fsdp", scatter_dimension=0, tiled=True
                ).astype(jnp.float32),
                lax.psum_scatter(
                    matrix_grads[1].astype(jnp.bfloat16), "fsdp", scatter_dimension=2, tiled=True
                ).astype(jnp.float32),
                lax.psum_scatter(
                    matrix_grads[2].astype(jnp.bfloat16), "fsdp", scatter_dimension=2, tiled=True
                ).astype(jnp.float32),
                lax.psum_scatter(
                    matrix_grads[3].astype(jnp.bfloat16), "fsdp", scatter_dimension=1, tiled=True
                ).astype(jnp.float32),
                lax.psum_scatter(
                    matrix_grads[4].astype(jnp.bfloat16), "fsdp", scatter_dimension=0, tiled=True
                ).astype(jnp.float32),
                lax.psum_scatter(
                    matrix_grads[5].astype(jnp.bfloat16), "fsdp", scatter_dimension=0, tiled=True
                ).astype(jnp.float32),
            )
            vector_part = (
                lax.psum_scatter(vector_grads[0], ("fsdp", "tp"), scatter_dimension=1, tiled=True),
                lax.psum_scatter(vector_grads[1], ("fsdp", "tp"), scatter_dimension=1, tiled=True),
            )
            totals = add_trees(totals, (matrix_part, vector_part))
    matrix_total, vector_total = totals
    ends = jnp.stack(
        [
            jnp.where(first_section, outputs_back[batch], outputs_fwd[batch])
            for batch in range(batches)
        ],
        0,
    )[None]
    return (
        ends,
        vector_total[0][None],
        vector_total[1][None],
        matrix_total[0][None],
        matrix_total[1][None],
        matrix_total[2][None],
        matrix_total[3][None],
        matrix_total[4][None],
        matrix_total[5][None],
    )


def solution(mesh):
    placed = (
        P("pipe", None, ("fsdp", "tp"), None),
        P(None, "fsdp"),
        P("pipe", None, ("fsdp", "tp")),
        P("pipe", None, ("fsdp", "tp")),
        P("pipe", "fsdp", None, "tp", None),
        P("pipe", None, "tp", "fsdp"),
        P("pipe", "tp", None, "fsdp"),
        P("pipe", None, ("fsdp", "tp")),
        P("pipe", ("fsdp", "tp")),
        P("pipe", ("fsdp", "tp"), None),
    )
    return jax.shard_map(
        on_device,
        mesh=mesh,
        in_specs=placed,
        out_specs=(
            P("pipe", None, ("fsdp", "tp"), None),
            P("pipe", None, ("fsdp", "tp")),
            P("pipe", None, ("fsdp", "tp")),
            P("pipe", "fsdp", None, "tp", None),
            P("pipe", None, "tp", "fsdp"),
            P("pipe", "tp", None, "fsdp"),
            P("pipe", None, ("fsdp", "tp")),
            P("pipe", ("fsdp", "tp")),
            P("pipe", ("fsdp", "tp"), None),
        ),
        check_vma=False,
    )
```

profile of v0, /device:TPU:0, one launch (start us, length us, event | category | flops | bytes accessed | tf_op | source)
XLA Modules:
  0.0 2137.0 jit_solution(9564170451595993972)
XLA Ops:
  10.1 180.0 %all-gather.1 = bf16[1,4,768]{1,0,2:T(2,128)(2,1)S(1)} all-gather(bf16[1,4,12]{1,0,2:T(2,128)(2,1)S(1)} %copy.193), channel_id=3, replica_groups=mesh['pipe'=2,'fsdp'=16,'tp'=4] {'fsdp','tp'}, dimensions={2}, use_global_device_ids=true | all-gather | bytes 6240 | tf_op jit(solution)/shard_map/all_gather | solution.py:249
  190.5 10.8 slice_reduce_fusion
  201.4 171.5 %all-gather = bf16[1,2,768]{1,0,2:T(2,128)(2,1)S(1)} all-gather(bf16[1,2,12]{1,0,2:T(2,128)(2,1)S(1)} %copy.192), channel_id=2, replica_groups=mesh['pipe'=2,'fsdp'=16,'tp'=4] {'fsdp','tp'}, dimensions={2}, use_global_device_ids=true | all-gather | bytes 3120 | tf_op jit(solution)/shard_map/all_gather | solution.py:248
  373.3 4.6 slice_reduce_fusion.5
  382.7 20.2 all-gather.3
  403.2 24.4 %all-gather.4 = bf16[1,3,64,768]{2,3,1,0:T(8,128)(2,1)S(1)} all-gather(bf16[1,3,64,48]{2,3,1,0:T(8,128)(2,1)S(1)} %copy-done.65), channel_id=6, replica_groups=mesh['pipe'=2,'fsdp'=16,'tp'=4] {'fsdp'}, dimensions={3}, use_global_device_ids=true | all-gather | bytes 313344 | tf_op jit(solution)/shard_map/all_gather | solution.py:242
  427.9 23.6 %all-gather.2 = bf16[1,768,3,3,64]{4,1,3,2,0:T(8,128)(2,1)S(1)} all-gather(bf16[1,48,3,3,64]{4,1,3,2,0:T(8,128)(2,1)S(1)} %copy-done.59), channel_id=4, replica_groups=mesh['pipe'=2,'fsdp'=16,'tp'=4] {'fsdp'}, dimensions={1}, use_global_device_ids=true | all-gather | bytes 940032 | tf_op jit(solution)/shard_map/all_gather | solution.py:240
  460.0 4.1 reshape.307
  468.6 16.2 fusion
  494.2 38.3 %all-reduce = bf16[768]{0:T(1024)(128)(2,1)S(1)} all-reduce(bf16[768]{0:T(1024)(128)(2,1)S(1)} %dynamic-update-slice), channel_id=8, replica_groups=mesh['pipe'=2,'fsdp'=16,'tp'=4] {'fsdp'}, use_global_device_ids=true, to_apply=%add | all-reduce | flops 768 | bytes 3072
  534.2 27.0 %all-gather.35.cloned.1.call-done = bf16[1,768,768]{1,2,0:T(8,128)(2,1)} async-done(((bf16[1,768,48]{1,2,0:T(8,128)(2,1)}), bf16[1,768,768]{1,2,0:T(8,128)(2,1)}) %all-gather.35.cloned.1.call-update) | async-done | bytes 1179664 | tf_op jit(solution)/shard_map/all_gather | solution.py:243
  561.2 8.7 fusion.14
  570.0 35.8 %all-gather.37.cloned.1.call-done = bf16[1,768,768]{2,1,0:T(8,128)(2,1)} async-done(((bf16[1,48,768]{2,1,0:T(8,128)(2,1)}), bf16[1,768,768]{2,1,0:T(8,128)(2,1)}) %all-gather.37.cloned.1.call-update) | async-done | bytes 1179664 | tf_op jit(solution)/shard_map/all_gather | solution.py:245
  605.7 3.8 convolution_convert_fusion.10
  609.5 20.9 fusion.1
  639.5 23.2 %all-gather.43.cloned.1.call-done = bf16[4,197,768]{2,1,0:T(8,128)(2,1)} async-done(((bf16[1,197,768]{2,1,0:T(8,128)(2,1)}), bf16[4,197,768]{2,1,0:T(8,128)(2,1)}) %all-gather.43.cloned.1.call-update) | async-done | bytes 1210384 | tf_op jit(solution)/shard_map/all_gather | solution.py:40
  674.6 26.7 %fusion.2 = bf16[200,768]{1,0:T(8,128)(2,1)S(1)} fusion(bf16[788,768]{1,0:T(8,128)(2,1)} %convolution_convert_fusion.9), kind=kCustom, calls=%all-reduce-scatter.2 | all-reduce-scatter fusion | flops 614401 | bytes 1518080
  712.9 23.4 %all-gather.47.cloned.1.call-done = bf16[4,197,768]{2,1,0:T(8,128)(2,1)} async-done(((bf16[1,197,768]{2,1,0:T(8,128)(2,1)}), bf16[4,197,768]{2,1,0:T(8,128)(2,1)}) %all-gather.47.cloned.1.call-update) | async-done | bytes 1210384 | tf_op jit(solution)/shard_map/all_gather | solution.py:40
  738.9 11.9 fusion.21
  757.3 32.4 %fusion.218 = (bf16[200,768]{1,0:T(8,128)(2,1)}, bf16[200,768]{1,0:T(8,128)(2,1)}) fusion(bf16[788,768]{1,0:T(8,128)(2,1)} %convolution_convert_fusion.7, bf16[788,768]{1,0:T(8,128)(2,1)} %convolution_convert_fusion.8), kind=kCustom, calls=%all-reduce-scatter.14 | all-reduce-scatter fusion | flops 1228801 | bytes 3035648
  790.4 3.3 collective-permute-start.7
  796.6 4.0 concatenate.13
  802.6 4.0 concatenate.15
  820.5 14.3 all-gather.49.cloned.1.call-done
  862.2 3.4 bitcast_convert_fusion.2
  872.6 4.3 reshape.313
  886.1 32.4 %fusion.217 = (bf16[200,768]{1,0:T(8,128)(2,1)}, bf16[200,768]{1,0:T(8,128)(2,1)}) fusion(bf16[788,768]{1,0:T(8,128)(2,1)} %convolution_convert_fusion.6, bf16[788,768]{1,0:T(8,128)(2,1)} %bitcast_convert_fusion.2), kind=kCustom, calls=%all-reduce-scatter.13 | all-reduce-scatter fusion | flops 1228801 | bytes 3035648
  919.2 3.3 collective-permute-start.10
  923.4 4.0 concatenate.16
  933.5 4.9 collective-permute-start.8
  939.4 4.0 concatenate.14
  952.6 5.8 all-gather.55.cloned.1.call-done
  961.0 9.3 fusion.30
  970.3 15.5 all-gather.53.cloned.1.call-done
  988.5 5.7 fusion.239
  997.4 20.6 fusion.7
  1022.5 4.0 concatenate.17
  1033.0 4.6 reshape.315
  1043.0 15.9 all-gather.57.cloned.1.call-done
  1086.7 3.4 bitcast_convert_fusion.1
  1090.2 20.5 fusion.8
  1115.2 3.3 concatenate.18
  1127.5 25.6 %all-gather.59.cloned.1.call-done = bf16[4,197,768]{2,1,0:T(8,128)(2,1)} async-done(((bf16[1,197,768]{2,1,0:T(8,128)(2,1)}), bf16[4,197,768]{2,1,0:T(8,128)(2,1)}) %all-gather.59.cloned.1.call-update) | async-done | bytes 1210384 | tf_op jit(solution)/shard_map/all_gather | solution.py:50
  1155.7 4.2 fusion.238
  1163.2 19.8 fusion.9
  1194.2 4.2 convolution_convert_fusion.17
  1198.4 4.1 convolution_convert_fusion.16
  1202.6 4.2 convolution_convert_fusion.15
  1206.9 4.1 convolution_convert_fusion.14
  1211.1 4.3 convolution_convert_fusion.13
  1215.6 4.1 convolution_convert_fusion.12
  1241.1 5.1 convolution_convert_fusion.2
  1251.9 4.0 convolution_convert_fusion.3
  1258.2 3.4 convolution_convert_fusion.1
  1278.7 3.4 bitcast_convert_fusion
  1282.0 29.7 %fusion.216 = (bf16[200,768]{1,0:T(8,128)(2,1)S(1)}, bf16[200,768]{1,0:T(8,128)(2,1)S(1)}) fusion(bf16[788,768]{1,0:T(8,128)(2,1)} %convolution_convert_fusion.3, bf16[788,768]{1,0:T(8,128)(2,1)} %bitcast_convert_fusion), kind=kCustom, calls=%all-reduce-scatter.12 | all-reduce-scatter fusion | flops 1228801 | bytes 3035648
  1317.1 4.7 convolution_convert_fusion
  1321.9 74.8 %all-reduce.34 = (bf16[2,3,64]{2,0,1:T(2,128)(2,1)S(1)}, bf16[2,3,64]{2,0,1:T(2,128)(2,1)S(1)}, bf16[2,3,64]{2,0,1:T(2,128)(2,1)S(1)}, bf16[768]{0:T(1024)(128)(...) all-reduce(bf16[2,3,64]{2,0,1:T(2,128)(2,1)S(1)} %pad_maximum_fusio, ...), channel_id=33, replica_groups=mesh['pipe'=2,'fsdp'=16,'tp'=4] {'fsdp'}, use_global_device_ids=true, to_apply=%region_77.78.clone | all-reduce | flops 3456 | bytes 13824
  1403.1 343.2 %all-reduce.33 = (f32[2,768]{1,0:T(2,128)S(1)}, f32[4,768]{1,0:T(4,128)S(1)}) all-reduce(f32[2,768]{1,0:T(2,128)S(1)} %fusion.205, f32[4,768]{1,0:T(4,128)S(1)} %fusion.204), channel_id=26, replica_groups=mesh['pipe'=2,'fsdp'=16,'tp'=4] {'fsdp','tp'}, use_global_device_ids=true, to_apply=%region_47.48.clone | all-reduce | flops 4608 | bytes 36864
  1750.9 73.4 %reduce-scatter.50.cloned.1.call-done = bf16[3,64,48]{1,2,0:T(8,128)(2,1)} async-done(((bf16[3,64,768]{1,2,0:T(8,128)(2,1)}), bf16[3,64,48]{1,2,0:T(8,128)(2,1)}) %reduce-scatter.50.cloned.1.call-update) | async-done | bytes 18448 | tf_op jit(solution)/shard_map/reduce_scatter | solution.py:299
  1824.3 74.5 %reduce-scatter.52.cloned.1.call-done = bf16[3,64,48]{1,2,0:T(8,128)(2,1)} async-done(((bf16[3,64,768]{1,2,0:T(8,128)(2,1)}), bf16[3,64,48]{1,2,0:T(8,128)(2,1)}) %reduce-scatter.52.cloned.1.call-update) | async-done | bytes 18448 | tf_op jit(solution)/shard_map/reduce_scatter | solution.py:299
  1900.3 75.0 %reduce-scatter.42.cloned.1.call-done = bf16[48,3,3,64]{3,0,2,1:T(8,128)(2,1)} async-done(((bf16[768,3,3,64]{3,0,2,1:T(8,128)(2,1)}), bf16[48,3,3,64]{3,0,2,1:T(8,128)(2,1)}) %reduce-scatter.42.cloned.1.call-update) | async-done | bytes 55312 | tf_op jit(solution)/shard_map/reduce_scatter | solution.py:293
  1975.3 76.5 %reduce-scatter.44.cloned.1.call-done = bf16[48,3,3,64]{3,0,2,1:T(8,128)(2,1)} async-done(((bf16[768,3,3,64]{3,0,2,1:T(8,128)(2,1)}), bf16[48,3,3,64]{3,0,2,1:T(8,128)(2,1)}) %reduce-scatter.44.cloned.1.call-update) | async-done | bytes 55312 | tf_op jit(solution)/shard_map/reduce_scatter | solution.py:293
  2051.8 76.5 %reduce-scatter.46.cloned.1.call-done = bf16[48,3,3,64]{3,0,2,1:T(8,128)(2,1)} async-done(((bf16[768,3,3,64]{3,0,2,1:T(8,128)(2,1)}), bf16[48,3,3,64]{3,0,2,1:T(8,128)(2,1)}) %reduce-scatter.46.cloned.1.call-update) | async-done | bytes 55312 | tf_op jit(solution)/shard_map/reduce_scatter | solution.py:293
  (579 shorter events, 300.7 us)
Async XLA Ops:
  7.2 370.7 %copy-start.38 = (bf16[1,2,197,768]{3,1,2,0:T(2,128)(2,1)S(1)}, bf16[1,2,197,768]{3,1,2,0:T(2,128)(2,1)}, u32[]{:S(2)}) copy-start(bf16[1,2,197,768]{3,1,2,0:T(2,128)(2,1)} %param.10) | copy-start | bytes 1815556
  7.2 446.0 %all-gather.39.cloned.1.call-start = ((), (), s32[]{:S(2)}) async-start(), calls=%async_computation.26 | async-start | bytes 1536000 | tf_op jit(solution)/shard_map/all_gather | solution.py:40
  201.4 918.9 %copy-start.60 = (f32[768]{0:T(1024)}, f32[768]{0:T(1024)S(1)}, u32[]{:S(2)}) copy-start(f32[768]{0:T(1024)S(1)} %get-tuple-element.57) | copy-start | bytes 9220
  377.9 742.3 %copy-start.56 = (f32[768]{0:T(1024)}, f32[768]{0:T(1024)S(1)}, u32[]{:S(2)}) copy-start(f32[768]{0:T(1024)S(1)} %get-tuple-element.61) | copy-start | bytes 9220
  380.3 71.2 %copy-start.69 = (f32[197]{0:T(256)}, f32[197]{0:T(256)S(1)}, u32[]{:S(2)}) copy-start(f32[197]{0:T(256)S(1)} %compare_convert_fusion.1) | copy-start | bytes 2368
  381.3 70.2 %copy-start.71 = (f32[197]{0:T(256)}, f32[197]{0:T(256)S(1)}, u32[]{:S(2)}) copy-start(f32[197]{0:T(256)S(1)} %broadcast_multiply_fusion.17) | copy-start | bytes 2368
  381.6 71.5 %copy-start.75 = (f32[197]{0:T(256)}, f32[197]{0:T(256)S(1)}, u32[]{:S(2)}) copy-start(f32[197]{0:T(256)S(1)} %add_rsqrt_fusion.5) | copy-start | bytes 2368
  382.5 150.1 %all-gather.41.cloned.1.call-start = ((), (), s32[]{:S(2)}) async-start(), calls=%async_computation.27 | async-start | bytes 1536000 | tf_op jit(solution)/shard_map/all_gather | solution.py:40
  427.9 244.2 %copy-start.23 = (bf16[1,3,64,768]{3,2,1,0:T(8,128)(2,1)}, bf16[1,3,64,768]{3,2,1,0:T(8,128)(2,1)S(1)}, u32[]{:S(2)}) copy-start(bf16[1,3,64,768]{3,2,1,0:T(8,128)(2,1)S(1)} %copy.203) | copy-start | bytes 884740
  484.9 4.3 collective-permute-start.4
  489.7 145.0 %copy-start.8 = (bf16[209,768]{1,0:T(8,128)(2,1)}, bf16[209,768]{1,0:T(8,128)(2,1)S(1)}, u32[]{:S(2)}) copy-start(bf16[209,768]{1,0:T(8,128)(2,1)S(1)} %concatenate.10) | copy-start | bytes 963076
  489.9 80.0 %copy-start.77 = (f32[197]{0:T(256)}, f32[197]{0:T(256)S(1)}, u32[]{:S(2)}) copy-start(f32[197]{0:T(256)S(1)} %broadcast_multiply_fusion.16) | copy-start | bytes 2368
  490.3 79.7 %copy-start.102 = (f32[197]{0:T(256)}, f32[197]{0:T(256)S(1)}, u32[]{:S(2)}) copy-start(f32[197]{0:T(256)S(1)} %multiply_reduce_fusion.10) | copy-start | bytes 2368
  490.3 79.7 %copy-start.100 = (f32[197]{0:T(256)}, f32[197]{0:T(256)S(1)}, u32[]{:S(2)}) copy-start(f32[197]{0:T(256)S(1)} %add_rsqrt_fusion.4) | copy-start | bytes 2368
  491.3 69.9 %all-gather.35.cloned.1.call-start = ((), (), s32[]{:S(2)}) async-start(), calls=%async_computation.24 | async-start | bytes 1253376 | tf_op jit(solution)/shard_map/all_gather | solution.py:243
  492.1 113.7 %all-gather.37.cloned.1.call-start = ((), (), s32[]{:S(2)}) async-start(), calls=%async_computation.25 | async-start | bytes 1253376 | tf_op jit(solution)/shard_map/all_gather | solution.py:245
  492.6 170.0 %all-gather.43.cloned.1.call-start = ((), (), s32[]{:S(2)}) async-start(), calls=%async_computation.28 | async-start | bytes 1536000 | tf_op jit(solution)/shard_map/all_gather | solution.py:40
  630.4 3.8 collective-permute-start.5
  635.0 2.5 collective-permute-start
  638.8 71.4 %all-gather.45.cloned.1.call-start = ((), (), s32[]{:S(2)}) async-start(), calls=%async_computation.29 | async-start | bytes 1536000 | tf_op jit(solution)/shard_map/all_gather | solution.py:50
  639.4 96.9 %all-gather.47.cloned.1.call-start = ((), (), s32[]{:S(2)}) async-start(), calls=%async_computation.30 | async-start | bytes 1536000 | tf_op jit(solution)/shard_map/all_gather | solution.py:40
  701.3 3.2 collective-permute-start.6
  710.0 124.8 %all-gather.49.cloned.1.call-start = ((), (), s32[]{:S(2)}) async-start(), calls=%async_computation.31 | async-start | bytes 1536000 | tf_op jit(solution)/shard_map/all_gather | solution.py:50
  790.4 6.1 collective-permute-start.7
  794.5 8.1 collective-permute-start.9
  811.1 54.5 %all-gather.51.cloned.1.call-start = ((), (), s32[]{:S(2)}) async-start(), calls=%async_computation.32 | async-start | bytes 1536000 | tf_op jit(solution)/shard_map/all_gather | solution.py:40
  811.1 4.7 collective-permute-start.2
  820.0 138.4 %all-gather.55.cloned.1.call-start = ((), (), s32[]{:S(2)}) async-start(), calls=%async_computation.34 | async-start | bytes 1536000 | tf_op jit(solution)/shard_map/all_gather | solution.py:40
  919.2 4.2 collective-permute-start.10
  932.7 53.1 %all-gather.53.cloned.1.call-start = ((), (), s32[]{:S(2)}) async-start(), calls=%async_computation.33 | async-start | bytes 1536000 | tf_op jit(solution)/shard_map/all_gather | solution.py:50
  933.5 5.8 collective-permute-start.8
  947.4 3.5 collective-permute-start.1
  949.4 79.9 %copy-start.73 = (f32[197]{0:T(256)}, f32[197]{0:T(256)S(1)}, u32[]{:S(2)}) copy-start(f32[197]{0:T(256)S(1)} %compare_convert_fusion) | copy-start | bytes 2368
  952.5 106.3 %all-gather.57.cloned.1.call-start = ((), (), s32[]{:S(2)}) async-start(), calls=%async_computation.35 | async-start | bytes 1536000 | tf_op jit(solution)/shard_map/all_gather | solution.py:50
  1018.7 3.8 collective-permute-start.11
  1033.0 120.1 %all-gather.59.cloned.1.call-start = ((), (), s32[]{:S(2)}) async-start(), calls=%async_computation.36 | async-start | bytes 1536000 | tf_op jit(solution)/shard_map/all_gather | solution.py:50
  1111.4 3.7 collective-permute-start.12
  1123.0 3.5 collective-permute-start.3
  1127.3 105.3 %all-gather.61.cloned.1.call-start = ((), (), s32[]{:S(2)}) async-start(), calls=%async_computation.37 | async-start | bytes 1536000 | tf_op jit(solution)/shard_map/all_gather | solution.py:50
  1183.1 3.8 collective-permute-start.13
  1194.1 553.5 %reduce-scatter.54.cloned.1.call-start = ((), (), s32[]{:S(2)}) async-start(), calls=%async_computation.18 | async-start | bytes 1253376 | tf_op jit(solution)/shard_map/reduce_scatter | solution.py:302
  1198.4 549.2 %reduce-scatter.56.cloned.1.call-start = ((), (), s32[]{:S(2)}) async-start(), calls=%async_computation.19 | async-start | bytes 1253376 | tf_op jit(solution)/shard_map/reduce_scatter | solution.py:302
  1202.6 545.1 %reduce-scatter.58.cloned.1.call-start = ((), (), s32[]{:S(2)}) async-start(), calls=%async_computation.20 | async-start | bytes 1253376 | tf_op jit(solution)/shard_map/reduce_scatter | solution.py:302
  1206.8 542.4 %reduce-scatter.60.cloned.1.call-start = ((), (), s32[]{:S(2)}) async-start(), calls=%async_computation.21 | async-start | bytes 1253376 | tf_op jit(solution)/shard_map/reduce_scatter | solution.py:308
  1211.0 538.2 %reduce-scatter.62.cloned.1.call-start = ((), (), s32[]{:S(2)}) async-start(), calls=%async_computation.22 | async-start | bytes 1253376 | tf_op jit(solution)/shard_map/reduce_scatter | solution.py:308
  1215.4 533.9 %reduce-scatter.64.cloned.1.call-start = ((), (), s32[]{:S(2)}) async-start(), calls=%async_computation.23 | async-start | bytes 1253376 | tf_op jit(solution)/shard_map/reduce_scatter | solution.py:308
  1219.8 531.1 %reduce-scatter.48.cloned.1.call-start = ((), (), s32[]{:S(2)}) async-start(), calls=%async_computation.15 | async-start | bytes 626688 | tf_op jit(solution)/shard_map/reduce_scatter | solution.py:299
  1225.8 598.6 %reduce-scatter.50.cloned.1.call-start = ((), (), s32[]{:S(2)}) async-start(), calls=%async_computation.16 | async-start | bytes 626688 | tf_op jit(solution)/shard_map/reduce_scatter | solution.py:299
  1232.5 666.3 %reduce-scatter.52.cloned.1.call-start = ((), (), s32[]{:S(2)}) async-start(), calls=%async_computation.17 | async-start | bytes 626688 | tf_op jit(solution)/shard_map/reduce_scatter | solution.py:299
  1238.4 736.9 %reduce-scatter.42.cloned.1.call-start = ((), (), s32[]{:S(2)}) async-start(), calls=%async_computation.12 | async-start | bytes 1880064 | tf_op jit(solution)/shard_map/reduce_scatter | solution.py:293
  1246.2 805.6 %reduce-scatter.44.cloned.1.call-start = ((), (), s32[]{:S(2)}) async-start(), calls=%async_computation.13 | async-start | bytes 1880064 | tf_op jit(solution)/shard_map/reduce_scatter | solution.py:293
  1261.7 866.7 %reduce-scatter.46.cloned.1.call-start = ((), (), s32[]{:S(2)}) async-start(), calls=%async_computation.14 | async-start | bytes 1880064 | tf_op jit(solution)/shard_map/reduce_scatter | solution.py:293
  1311.7 86.2 %collective-permute-start.14 = (bf16[9,768]{1,0:T(8,128)(2,1)S(1)}, bf16[9,768]{1,0:T(8,128)(2,1)S(1)}, u32[]{:S(2)}, u32[]{:S(2)}) collective-permute-start(bf16[9,768]{1,0:T(8,128)(2,1)S(1)} %slice.204), channel_id=1, source_target_pairs={{0,1},{1,2},{2,3},{4,5},{5,6},{6,7},{8,9},{9,10},{10,11},{12,13},{... | collective-permute-start | bytes 41480
  1314.3 84.9 %collective-permute-start.15 = (bf16[9,768]{1,0:T(8,128)(2,1)S(1)}, bf16[9,768]{1,0:T(8,128)(2,1)S(1)}, u32[]{:S(2)}, u32[]{:S(2)}) collective-permute-start(bf16[9,768]{1,0:T(8,128)(2,1)S(1)} %slice.205), channel_id=1, source_target_pairs={{0,1},{1,2},{2,3},{4,5},{5,6},{6,7},{8,9},{9,10},{10,11},{12,13},{... | collective-permute-start | bytes 41480
  1321.8 76.7 %copy-start.3 = (bf16[197,768]{1,0:T(8,128)(2,1)S(1)}, bf16[197,768]{1,0:T(8,128)(2,1)}, u32[]{:S(2)}) copy-start(bf16[197,768]{1,0:T(8,128)(2,1)} %copy-done.1) | copy-start | bytes 907780
  1321.8 76.7 %copy-start.5 = (bf16[197,768]{1,0:T(8,128)(2,1)S(1)}, bf16[197,768]{1,0:T(8,128)(2,1)}, u32[]{:S(2)}) copy-start(bf16[197,768]{1,0:T(8,128)(2,1)} %copy-done.4) | copy-start | bytes 907780
  1321.8 76.7 %copy-start.37 = (bf16[197,768]{1,0:T(8,128)(2,1)S(1)}, bf16[197,768]{1,0:T(8,128)(2,1)}, u32[]{:S(2)}) copy-start(bf16[197,768]{1,0:T(8,128)(2,1)} %copy-done.36) | copy-start | bytes 907780
  1321.8 76.7 %copy-start.57 = (f32[768]{0:T(1024)S(1)}, f32[768]{0:T(1024)}, u32[]{:S(2)}) copy-start(f32[768]{0:T(1024)} %copy-done.56) | copy-start | bytes 9220
  1321.8 76.7 %copy-start.64 = (f32[197]{0:T(256)S(1)}, f32[197]{0:T(256)}, u32[]{:S(2)}) copy-start(f32[197]{0:T(256)} %copy-done.62) | copy-start | bytes 2368
  1321.8 76.7 %copy-start.68 = (f32[197]{0:T(256)S(1)}, f32[197]{0:T(256)}, u32[]{:S(2)}) copy-start(f32[197]{0:T(256)} %copy-done.66) | copy-start | bytes 2368
  1321.8 76.7 %copy-start.74 = (f32[197]{0:T(256)S(1)}, f32[197]{0:T(256)}, u32[]{:S(2)}) copy-start(f32[197]{0:T(256)} %copy-done.73) | copy-start | bytes 2368
  1321.8 78.0 %copy-start.9 = (bf16[209,768]{1,0:T(8,128)(2,1)S(1)}, bf16[209,768]{1,0:T(8,128)(2,1)}, u32[]{:S(2)}) copy-start(bf16[209,768]{1,0:T(8,128)(2,1)} %concatenate.16) | copy-start | bytes 963076
  1321.8 78.0 %copy-start.21 = (f32[197,768]{1,0:T(8,128)S(1)}, f32[197,768]{1,0:T(8,128)}, u32[]{:S(2)}) copy-start(f32[197,768]{1,0:T(8,128)} %copy-done.20) | copy-start | bytes 1815556
  1321.9 78.0 %copy-start.61 = (f32[768]{0:T(1024)S(1)}, f32[768]{0:T(1024)}, u32[]{:S(2)}) copy-start(f32[768]{0:T(1024)} %copy-done.60) | copy-start | bytes 9220
  (103 other events, 1123.8 us)
Sparse Core Ops, SparseCore 0:
  382.6 19.9 all-gather.38
  491.5 23.7 all-gather.40
  517.4 43.8 all-gather.34
  563.2 42.4 all-gather.36
  639.0 23.6 all-gather.42
  664.1 30.5 all-gather.44
  710.1 26.1 all-gather.46
  811.2 23.5 all-gather.48
  836.4 25.1 all-gather.50
  932.9 25.4 all-gather.54
  960.6 25.1 all-gather.52
  1033.1 25.7 all-gather.56
  1127.4 25.6 all-gather.58
  1194.2 25.6 all-gather.60
  1223.0 73.9 reduce-scatter.53
  1300.0 72.5 reduce-scatter.55
  1375.7 72.6 reduce-scatter.57
  1451.4 72.5 reduce-scatter.59
  1527.2 72.5 reduce-scatter.61
  1602.9 72.5 reduce-scatter.63
  1678.7 71.1 reduce-scatter.47
  1753.1 71.2 reduce-scatter.49
  1827.5 71.2 reduce-scatter.51
  1902.0 73.2 reduce-scatter.41
  1978.6 73.1 reduce-scatter.43
  2055.0 73.2 reduce-scatter.45
where the time goes:
time: 2150 us; the launch traced here: 2140 us
  blocking collectives  1100 us (51%)
  waiting for transfers between devices  578 us (27%)
  local copies, waits for them, and re-layouts  179 us (8%)
  matrix products  157 us (7%)
  other arithmetic  66.6 us (3%)
  starting transfers between devices  41.2 us (2%)
    unnamed x12, blocking collectives  675 us
    reduce_scatter x3, waiting for transfers between devices, on_device(): lax.psum_scatter(matrix_grads[0].astype(jnp.bfloat16), 'fsdp', scatter_di...  228 us
    all_gather x1, blocking collectives, fetch(): lax.all_gather(vector_shards[1], ('fsdp', 'tp'), axis=1, tiled=True)  180 us
    all_gather x1, blocking collectives, fetch(): lax.all_gather(vector_shards[0], ('fsdp', 'tp'), axis=1, tiled=True)  172 us
    reduce_scatter x3, waiting for transfers between devices, on_device(): lax.psum_scatter(matrix_grads[2].astype(jnp.bfloat16), 'fsdp', scatter_di...  148 us
    unnamed x300, local copies, waits for them, and re-layouts  93.9 us
    all_gather x6, waiting for transfers between devices, spread_grads(): return lax.all_gather(values, 'tp', axis=0, tiled=True)  71.3 us
    all_gather x6, waiting for transfers between devices, spread_rows(): return lax.all_gather(values, 'tp', axis=0, tiled=True)  52.4 us
  transfers between devices with their start and end apart: 42, of which 25 were waited for; matrix products, arithmetic and copies ran while one was open for 12% of the time, Pallas kernels for 0%

commit v1 on v0

v1 whole, which is shorter than its diff:
```python
import types

import jax
import jax.numpy as jnp
from jax import lax
from jax.experimental import pallas as pl
from jax.experimental.pallas import tpu as pltpu
from jax.sharding import PartitionSpec as P

MESH = pl.DeviceIdType.MESH
bf16 = jnp.bfloat16
f32 = jnp.float32


ORDERS = (("x", "y", "z"), ("y", "z", "x"), ("z", "x", "y"))
LAYOUT = (("x", "z", "y"), ("z", "y", "x"), ("z", "y", "x"))


def place():
    f = lax.axis_index("fsdp")
    return {"z": f // 4, "y": lax.rem(f, 4), "x": lax.axis_index("tp")}


def device_at(coords):
    return {"fsdp": coords["z"] * 4 + coords["y"], "tp": coords["x"]}


def moved(coords, axis, by):
    out = dict(coords)
    out[axis] = lax.rem(coords[axis] + by, 4)
    return out


def sibling():
    return {"pipe": 1 - lax.axis_index("pipe")}


def enter(coords):
    barrier = pltpu.get_barrier_semaphore()
    for axis in ("x", "y", "z"):
        for by in (1, 2, 3):
            pl.semaphore_signal(barrier, inc=1, device_id=device_at(moved(coords, axis, by)), device_id_type=MESH)
    pl.semaphore_signal(barrier, inc=1, device_id=sibling(), device_id_type=MESH)
    pl.semaphore_wait(barrier, 10)


def block_of(buf, coords, kind, third, free, axis, value, half):
    index, cols = [], slice(None)
    uncut = half is not None
    for name in LAYOUT[kind]:
        if name in free:
            index.append(pl.ds(half * 2, 2) if uncut else slice(None))
            uncut = False
        else:
            index.append(value if name == axis else coords[name])
    if uncut:
        cols = pl.ds(half * 384, 384)
    return buf.at[(kind, *index, pl.ds(third * 16, 16), cols)]


class Gather:
    def __init__(self, buf, kind, third, coords, send, recv):
        self.buf, self.kind, self.third, self.coords = buf, kind, third, coords
        self.send, self.recv, self.sid = send, recv, kind * 3 + third

    def copy(self, phase, which):
        order = ORDERS[self.third]
        axis = order[phase]
        me = self.coords[axis]
        value = (me, me, lax.rem(me + 3, 4), lax.rem(me + 1, 4))[which]
        ref = block_of(
            self.buf, self.coords, self.kind, self.third, order[:phase], axis, value, (None, None, 0, 1)[which]
        )
        return pltpu.make_async_remote_copy(
            src_ref=ref,
            dst_ref=ref,
            send_sem=self.send.at[self.sid, phase, which],
            recv_sem=self.recv.at[self.sid, phase, which],
            device_id=device_at(moved(self.coords, axis, (1, 3)[which % 2])),
            device_id_type=MESH,
        )

    def step(self, number):
        phase, stage = number // 3, number % 3
        if stage == 0:
            self.copy(phase, 0).start()
            self.copy(phase, 1).start()
        elif stage == 1:
            self.copy(phase, 0).wait_recv()
            self.copy(phase, 2).start()
            self.copy(phase, 1).wait_recv()
            self.copy(phase, 3).start()
        else:
            self.copy(phase, 2).wait_recv()
            self.copy(phase, 3).wait_recv()

    def drain(self):
        for phase in range(3):
            for which in range(4):
                self.copy(phase, which).wait_send()


class Scatter:
    def __init__(self, buf, kind, third, coords, landings, send, recv, out):
        self.buf, self.kind, self.third, self.coords = buf, kind, third, coords
        self.landings, self.send, self.recv, self.sid, self.out = landings, send, recv, kind * 3 + third, out

    def block(self, phase, by, half):
        order = ORDERS[self.third][::-1]
        axis = order[phase]
        value = lax.rem(self.coords[axis] + by, 4)
        return block_of(self.buf, self.coords, self.kind, self.third, order[phase + 1 :], axis, value, half)

    def landing(self, phase, which):
        return self.landings[2 * phase + which // 2].at[self.sid, which % 2]

    def copy(self, phase, which):
        axis = ORDERS[self.third][::-1][phase]
        by = (2, 2, 1, 3)[which]
        return pltpu.make_async_remote_copy(
            src_ref=self.block(phase, by, (0, 1, None, None)[which]),
            dst_ref=self.landing(phase, which),
            send_sem=self.send.at[self.sid, phase, which],
            recv_sem=self.recv.at[self.sid, phase, which],
            device_id=device_at(moved(self.coords, axis, (1, 3)[which % 2])),
            device_id_type=MESH,
        )

    def step(self, number):
        phase, stage = number // 3, number % 3
        if stage == 0:
            self.copy(phase, 0).start()
            self.copy(phase, 1).start()
        elif stage == 1:
            for which, by in ((0, 1), (1, 3)):
                self.copy(phase, which).wait_recv()
                mine = self.block(phase, by, which)
                mine[...] = (mine[...].astype(f32) + self.landing(phase, which)[...].astype(f32)).astype(bf16)
                self.copy(phase, 2 + which).start()
        else:
            self.copy(phase, 2).wait_recv()
            self.copy(phase, 3).wait_recv()
            mine = self.block(phase, 0, None)
            total = (
                mine[...].astype(f32)
                + self.landing(phase, 2)[...].astype(f32)
                + self.landing(phase, 3)[...].astype(f32)
            )
            if phase < 2:
                mine[...] = total.astype(bf16)
            else:
                self.out[pl.ds(self.kind * 48 + self.third * 16, 16), :] = total

    def drain(self):
        for phase in range(3):
            for which in range(4):
                self.copy(phase, which).wait_send()


class AllSum:
    def __init__(self, stages, landings, coords, send, recv):
        self.stages, self.landings, self.coords, self.send, self.recv = stages, landings, coords, send, recv

    def copy(self, phase, which):
        return pltpu.make_async_remote_copy(
            src_ref=self.stages.at[phase],
            dst_ref=self.landings.at[phase, which],
            send_sem=self.send.at[phase, which],
            recv_sem=self.recv.at[phase, which],
            device_id=device_at(moved(self.coords, "xyz"[phase], which + 1)),
            device_id_type=MESH,
        )

    def start(self, phase):
        for which in range(3):
            self.copy(phase, which).start()

    def finish(self, phase):
        for which in range(3):
            self.copy(phase, which).wait_recv()
        self.stages[phase + 1] = (self.stages[phase] + self.landings[phase, 0]) + (
            self.landings[phase, 1] + self.landings[phase, 2]
        )

    def drain(self):
        for phase in range(3):
            for which in range(3):
                self.copy(phase, which).wait_send()


LANDINGS = [
    pltpu.VMEM((9, 2, 2, 4, 16, 768), bf16),
    pltpu.VMEM((9, 2, 4, 4, 16, 768), bf16),
    pltpu.VMEM((9, 2, 2, 16, 768), bf16),
    pltpu.VMEM((9, 2, 4, 16, 768), bf16),
    pltpu.VMEM((9, 2, 16, 384), bf16),
    pltpu.VMEM((9, 2, 16, 768), bf16),
]


SEQ, IMG, ROWS = 197, 208, 416
CHUNK = 32
EPS = 1e-6


def nn(a, b):
    return jnp.dot(a, b, preferred_element_type=f32)


def nt(a, b):
    return lax.dot_general(a, b, (((1,), (1,)), ((), ())), preferred_element_type=f32)


def tn(a, b):
    return lax.dot_general(a, b, (((0,), (0,)), ((), ())), preferred_element_type=f32)


def normed(v):
    center = v - jnp.mean(v, -1, keepdims=True)
    inv = lax.rsqrt(jnp.mean(center * center, -1, keepdims=True) + EPS)
    return center * inv, inv


def norm_back(dn, xhat, inv, gain):
    scaled = dn * gain
    return inv * (scaled - jnp.mean(scaled, -1, keepdims=True)
                  - xhat * jnp.mean(scaled * xhat, -1, keepdims=True))


def fold(v):
    return jnp.sum(v.reshape(v.shape[0] // 8, 8, v.shape[1]), axis=0)


def row_loop(body, init=None):
    def step(i, carry):
        return body(pl.ds(pl.multiple_of(i * CHUNK, CHUNK), CHUNK), carry)
    return lax.fori_loop(0, ROWS // CHUNK, step, init)


def square(ref, kind, j, lo=0, hi=768):
    return ref[kind, j, :, :, :, lo:hi].reshape(768, hi - lo)


def forward(r):
    vec = r.vec

    def first_norm(rows, _):
        xhat, _inv = normed(r.x[rows, :].astype(f32))
        r.n1[rows, :] = (xhat * vec[0:1, :] + vec[2:3, :]).astype(bf16)
    row_loop(first_norm)

    low = lax.broadcasted_iota(jnp.int32, (IMG, 128), 1) < 64
    keyed = lax.broadcasted_iota(jnp.int32, (IMG, IMG), 1) < SEQ
    zero = jnp.zeros((IMG, 128), bf16)

    def head_group(t, _):
        r.q[t] = (nn(r.n1[...], square(r.w, 0, t, 0, 640)) + vec[pl.ds(10 + t, 1), 0:640]).astype(bf16)

        def image(i, _):
            rows = pl.ds(pl.multiple_of(i * IMG, IMG), IMG)
            tq, tk, tv, t3, t4 = (r.q[t, rows, k * 128:(k + 1) * 128] for k in range(5))

            def probs(h, qs, ks):
                s = nt(qs, ks) * 0.125
                s = jnp.where(keyed, s, -1e30)
                e = jnp.exp(s - jnp.max(s, -1, keepdims=True))
                p = (e * (1.0 / jnp.sum(e, -1, keepdims=True))).astype(bf16)
                r.p[(t * 2 + i) * 3 + h] = p
                return p
            p0 = probs(0, jnp.where(low, tq, zero), tk)
            p1 = probs(1, jnp.where(low, zero, tq), tk)
            p2 = probs(2, jnp.where(low, t3, zero), t4)
            r.mx[t, rows, 0:128] = jnp.where(low, 0.0, nn(p2, t3)).astype(bf16)
            r.mx[t, rows, 128:256] = jnp.where(low, nn(p0, tv), nn(p1, tv)).astype(bf16)
            return 0
        lax.fori_loop(0, 2, image, 0)
        part = nt(r.mx[t], square(r.w, 0, t, 512, 768))

        @pl.when(t == 0)
        def _():
            r.acc[...] = part

        @pl.when(t > 0)
        def _():
            r.acc[...] += part
        return 0
    lax.fori_loop(0, 4, head_group, 0)

    def second_norm(rows, _):
        h1 = r.x[rows, :].astype(f32) + r.acc[rows, :] + vec[3:4, :]
        r.h1[rows, :] = h1
        xhat, _inv = normed(h1)
        r.n2[rows, :] = (xhat * vec[1:2, :] + vec[4:5, :]).astype(bf16)
        r.acc[rows, :] = h1 + vec[5:6, :]
    row_loop(second_norm)

    def hidden(j, _):
        r.tmp[...] = nt(r.n2[...], square(r.w, 1, j)) + vec[pl.ds(6 + j, 1), :]

        def gelu(rows, _):
            u = r.tmp[rows, :]
            cdf = 0.5 * (1.0 + lax.erf(u * 0.7071067811865476))
            r.act[j, rows, :] = (u * cdf).astype(bf16)
            r.gp[j, rows, :] = (cdf + u * (jnp.exp(-0.5 * u * u) * 0.3989422804014327)).astype(bf16)
        row_loop(gelu)
        r.acc[...] += nn(r.act[j], square(r.w, 2, j))
        return 0
    lax.fori_loop(0, 4, hidden, 0)


def backward_ffn(r):
    vec = r.vec
    dvec = r.dvec

    def hidden(j, _):
        r.tmp[...] = nt(r.gy[...], square(r.w, 2, j))

        def chain(rows, total):
            du = (r.tmp[rows, :] * r.gp[j, rows, :].astype(f32)).astype(bf16)
            r.dx[rows, :] = du
            return total + fold(du.astype(f32))
        total = row_loop(chain, jnp.zeros((8, 768), f32))
        dvec[pl.ds(6 + j, 1), :] = jnp.sum(total, 0, keepdims=True)
        r.g[2, j] = tn(r.act[j], r.gy[...]).astype(bf16).reshape(4, 4, 48, 768)
        r.g[1, j] = tn(r.dx[...], r.n2[...]).astype(bf16).reshape(4, 4, 48, 768)
        part = nn(r.dx[...], square(r.w, 1, j))

        @pl.when(j == 0)
        def _():
            r.acc[...] = part

        @pl.when(j > 0)
        def _():
            r.acc[...] += part
        return 0
    lax.fori_loop(0, 4, hidden, 0)

    def norm_two(rows, sums):
        dn = r.acc[rows, :]
        gy = r.gy[rows, :].astype(f32)
        xhat, inv = normed(r.h1[rows, :])
        dh = gy + norm_back(dn, xhat, inv, vec[1:2, :])
        r.tmp[rows, :] = dh
        gh = dh.astype(bf16)
        r.n2[rows, :] = gh
        return (sums[0] + fold(dn * xhat), sums[1] + fold(dn), sums[2] + fold(gh.astype(f32)), sums[3] + fold(gy))
    zero = jnp.zeros((8, 768), f32)
    sums = row_loop(norm_two, (zero,) * 4)
    for row, total in zip((1, 4, 3, 5), sums):
        dvec[row:row + 1, :] = jnp.sum(total, 0, keepdims=True)


def backward_attention(r):
    vec = r.vec
    dvec = r.dvec
    dqkv, dmixed = r.gp.at[0], r.gp.at[1]
    low = lax.broadcasted_iota(jnp.int32, (IMG, 128), 1) < 64
    zero = jnp.zeros((IMG, 128), bf16)

    def head_group(t, _):
        dmixed[:, 0:256] = nn(r.n2[...], square(r.w, 0, t, 512, 768)).astype(bf16)

        def image(i, _):
            rows = pl.ds(pl.multiple_of(i * IMG, IMG), IMG)
            tq, tk, tv, t3, t4 = (r.q[t, rows, k * 128:(k + 1) * 128] for k in range(5))
            d4 = dmixed[rows, 0:128]
            d5 = dmixed[rows, 128:256]

            def head(h, d_full, d_masked, v, q, k):
                p = r.p[(t * 2 + i) * 3 + h]
                pf = p.astype(f32)
                dv = tn(p, d_full)
                dp = nt(d_masked, v)
                ds = (pf * (dp - jnp.sum(dp * pf, -1, keepdims=True))).astype(bf16)
                return nn(ds, k) * 0.125, tn(ds, q) * 0.125, dv
            dq0, dk0, dv0 = head(0, d5, jnp.where(low, d5, zero), tv, tq, tk)
            dq1, dk1, dv1 = head(1, d5, jnp.where(low, zero, d5), tv, tq, tk)
            dqkv[rows, 0:128] = jnp.where(low, dq0, dq1).astype(bf16)
            dqkv[rows, 128:256] = jnp.where(low, dk0, dk1).astype(bf16)
            dqkv[rows, 256:384] = jnp.where(low, dv0, dv1).astype(bf16)
            dq2, dk2, dv2 = head(2, d4, jnp.where(low, zero, d4), t3, t3, t4)
            dqkv[rows, 384:512] = jnp.where(low, dq2, dv2).astype(bf16)
            dqkv[rows, 512:640] = jnp.where(low, dk2, 0.0).astype(bf16)
            return 0
        lax.fori_loop(0, 2, image, 0)
        dvec[pl.ds(10 + t, 1), 0:640] = jnp.sum(dqkv[:, 0:640].astype(f32), 0, keepdims=True)
        ga = tn(r.n1[...], dqkv[:, 0:640])
        go = tn(r.n2[...], r.mx[t])
        r.g[0, t, :, :, :, 0:512] = ga[:, 0:512].astype(bf16).reshape(4, 4, 48, 512)
        r.g[0, t, :, :, :, 512:640] = (ga[:, 512:640] + go[:, 0:128]).astype(bf16).reshape(4, 4, 48, 128)
        r.g[0, t, :, :, :, 640:768] = go[:, 128:256].astype(bf16).reshape(4, 4, 48, 128)
        part = nt(dqkv[:, 0:640], square(r.w, 0, t, 0, 640))

        @pl.when(t == 0)
        def _():
            r.acc[...] = part

        @pl.when(t > 0)
        def _():
            r.acc[...] += part
        return 0
    lax.fori_loop(0, 4, head_group, 0)

    def norm_one(rows, sums):
        dn = r.acc[rows, :]
        xhat, inv = normed(r.x[rows, :].astype(f32))
        dx = r.tmp[rows, :] + norm_back(dn, xhat, inv, vec[0:1, :])
        r.dx[rows, :] = dx.astype(bf16)
        return (sums[0] + fold(dn * xhat), sums[1] + fold(dn))
    zero = jnp.zeros((8, 768), f32)
    sums = row_loop(norm_one, (zero,) * 2)
    for row, total in zip((0, 2), sums):
        dvec[row:row + 1, :] = jnp.sum(total, 0, keepdims=True)


SLOTS = (3, 4, 4, 4, 48, 768)
BODY_SCRATCH = dict(
    x=pltpu.VMEM((ROWS, 768), bf16), n1=pltpu.VMEM((ROWS, 768), bf16), q=pltpu.VMEM((4, ROWS, 640), bf16),
    p=pltpu.VMEM((24, IMG, IMG), bf16), mx=pltpu.VMEM((4, ROWS, 256), bf16), acc=pltpu.VMEM((ROWS, 768), f32),
    h1=pltpu.VMEM((ROWS, 768), f32), n2=pltpu.VMEM((ROWS, 768), bf16), act=pltpu.VMEM((4, ROWS, 768), bf16),
    gp=pltpu.VMEM((4, ROWS, 768), bf16), tmp=pltpu.VMEM((ROWS, 768), f32), gy=pltpu.VMEM((ROWS, 768), bf16),

    dx=pltpu.VMEM((ROWS, 768), bf16),
    vec=pltpu.VMEM((16, 768), f32), dvec=pltpu.VMEM((16, 768), f32),
    w=pltpu.VMEM(SLOTS, bf16), g=pltpu.VMEM(SLOTS, bf16),
)


NAMES = list(BODY_SCRATCH)


def layer_kernel(w_hbm, rows_hbm, vec_hbm, end_hbm, grad_hbm, dvec_hbm, *scratch):
    r = types.SimpleNamespace(**dict(zip(NAMES, scratch)))
    rest = scratch[len(NAMES) :]
    landings, out = rest[:6], r.acc
    stages, sum_landings, ag_send, ag_recv, rs_send, rs_recv, sum_send, sum_recv, link, local = rest[6:]
    coords = place()
    first = lax.axis_index("pipe") == 0
    second = lax.axis_index("pipe") == 1
    enter(coords)

    own = [
        pltpu.make_async_copy(
            w_hbm.at[kind], r.w.at[(kind, *(coords[name] for name in LAYOUT[kind]))], local.at[kind]
        )
        for kind in range(3)
    ]
    for copy in own:
        copy.start()
    vec_in = pltpu.make_async_copy(vec_hbm, stages.at[0, 0], local.at[3])
    vec_in.start()

    @pl.when(first)
    def _():
        copy = pltpu.make_async_copy(rows_hbm, r.x, local.at[4])
        copy.start()
        copy.wait()

    @pl.when(second)
    def _():
        copy = pltpu.make_async_copy(rows_hbm, r.gy, local.at[4])
        copy.start()
        copy.wait()

    for copy in own:
        copy.wait()
    vec_in.wait()

    gathers = [Gather(r.w, kind, third, coords, ag_send, ag_recv) for kind in range(3) for third in range(3)]
    sums = [
        AllSum(stages.at[k], sum_landings.at[k], coords, sum_send.at[k], sum_recv.at[k]) for k in range(2)
    ]
    for number in range(9):
        for gather in gathers:
            gather.step(number)
        if number % 3 == 0:
            sums[0].start(number // 3)
        elif number % 3 == 1:
            sums[0].finish(number // 3)
    r.vec[...] = stages[0, 3]
    r.dvec[...] = jnp.zeros_like(r.dvec)
    for gather in gathers:
        gather.drain()
    sums[0].drain()

    up = pltpu.make_async_remote_copy(
        src_ref=r.dx, dst_ref=r.x, send_sem=link.at[0], recv_sem=link.at[1], device_id=sibling(), device_id_type=MESH
    )
    down = pltpu.make_async_remote_copy(
        src_ref=r.dx, dst_ref=r.gy, send_sem=link.at[2], recv_sem=link.at[3], device_id=sibling(), device_id_type=MESH
    )
    end = pltpu.make_async_copy(r.dx, end_hbm, local.at[5])

    @pl.when(second)
    def _():
        up.wait_recv()

    forward(r)
    r.dx[...] = r.acc[...].astype(bf16)

    @pl.when(first)
    def _():
        up.start()
        up.wait_send()
        down.wait_recv()

    @pl.when(second)
    def _():
        end.start()
        end.wait()

    backward_ffn(r)
    scatters = [
        Scatter(r.g, kind, third, coords, landings, rs_send, rs_recv, out) for kind in range(3) for third in range(3)
    ]
    for scatter in scatters[3:]:
        scatter.step(0)
    backward_attention(r)

    @pl.when(first)
    def _():
        end.start()
        end.wait()

    @pl.when(second)
    def _():
        down.start()
        down.wait_send()

    stages[1, 0] = r.dvec[...]
    for scatter in scatters[:3]:
        scatter.step(0)
    for number in range(9):
        for scatter in scatters:
            if number:
                scatter.step(number)
        if number % 3 == 0:
            sums[1].start(number // 3)
        elif number % 3 == 1:
            sums[1].finish(number // 3)
    for scatter in scatters:
        scatter.drain()
    sums[1].drain()
    copies = [
        pltpu.make_async_copy(out.at[pl.ds(0, 144)], grad_hbm, local.at[0]),
        pltpu.make_async_copy(stages.at[1, 3], dvec_hbm, local.at[1]),
    ]
    for copy in copies:
        copy.start()
    for copy in copies:
        copy.wait()


def units(q, k, v, o):
    order = ((q, 0), (q, 1), (k, 0), (k, 1), (v, 0), (v, 1), (q, 2), (v, 2), (k, 2), (o, 2), (o, 0), (o, 1))
    return jnp.concatenate([a[..., h, :] for a, h in order], -1)


def split_units(joined):
    part = [joined[..., 64 * n : 64 * n + 64] for n in range(joined.shape[-1] // 64)]
    pick = lambda *numbers: jnp.stack([part[n] for n in numbers], -2)
    return pick(0, 1, 6), pick(2, 3, 8), pick(4, 5, 7), (pick(10, 11, 9) if len(part) > 10 else None)


def on_device(
    boundary, loads, norm_gains, row_biases, w_qkv, qv_bias, w_out, w_up, up_bias, w_down
):
    first = lax.axis_index("pipe") == 0
    fsdp, tp = lax.axis_index("fsdp"), lax.axis_index("tp")
    chip = fsdp * 4 + tp
    live = (tp < loads[:, 0])[:, None, None]
    rows = jnp.where(first | live, boundary[0], 0)
    rows = jnp.pad(rows, ((0, 0), (0, IMG - SEQ), (0, 0))).reshape(ROWS, 768)

    wq = w_qkv[0]
    wo = w_out[0].transpose(2, 0, 1)
    weights = jnp.stack([units(wq[:, 0], wq[:, 1], wq[:, 2], wo), w_up[0].T, w_down[0]], 0)

    lanes = jnp.arange(768, dtype=jnp.int32)
    small = jnp.concatenate([norm_gains[0], row_biases[0]], 0).astype(f32)
    small = jnp.where(lanes // 12 == chip, jnp.tile(small, (1, 64)), 0.0)
    hidden = jnp.arange(3072, dtype=jnp.int32)
    hidden = jnp.where(hidden // 48 == chip, jnp.tile(up_bias[0].astype(f32), 64), 0.0).reshape(4, 768)
    heads = jnp.where(
        jnp.arange(64, dtype=jnp.int32) // 4 == fsdp, jnp.tile(qv_bias[0].astype(f32), (1, 1, 16)), 0.0
    )
    none = jnp.zeros_like(heads[0])
    heads = units(heads[0], none, heads[1], none)
    heads = jnp.where(jnp.arange(4, dtype=jnp.int32)[:, None] == tp, heads[None], 0.0)
    vec = jnp.concatenate([small, hidden, heads, jnp.zeros((2, 768), f32)], 0)

    anywhere = pl.BlockSpec(memory_space=pl.ANY)
    dma = pltpu.SemaphoreType.DMA
    end, grads, dvec = pl.pallas_call(
        layer_kernel,
        out_shape=(
            jax.ShapeDtypeStruct((ROWS, 768), bf16),
            jax.ShapeDtypeStruct((144, 768), f32),
            jax.ShapeDtypeStruct((16, 768), f32),
        ),
        in_specs=[anywhere] * 3,
        out_specs=(anywhere,) * 3,
        scratch_shapes=[
            *BODY_SCRATCH.values(),
            *LANDINGS,
            pltpu.VMEM((2, 4, 16, 768), f32),
            pltpu.VMEM((2, 3, 3, 16, 768), f32),
            dma((9, 3, 4)),
            dma((9, 3, 4)),
            dma((9, 3, 4)),
            dma((9, 3, 4)),
            dma((2, 3, 3)),
            dma((2, 3, 3)),
            dma((4,)),
            dma((6,)),
        ],
        compiler_params=pltpu.CompilerParams(
            collective_id=0, has_side_effects=True, vmem_limit_bytes=63 * 2**20
        ),
    )(weights, rows, vec)

    end = end.reshape(2, IMG, 768)[:, :SEQ]
    ends = jnp.where(first | live, end, 0)[None]
    gq, gk, gv, go = split_units(grads[:48])
    mine = lax.dynamic_slice(dvec, (0, chip * 12), (6, 12))
    up_row = lax.dynamic_slice(dvec[6:10].reshape(3072), (chip * 48,), (48,))
    head_row = lax.dynamic_slice(dvec, (10 + tp, 0), (1, 640))[0]
    hq, _, hv, _ = split_units(head_row)
    head_grads = lax.dynamic_slice(jnp.stack([hq, hv], 0), (0, 0, fsdp * 4), (2, 3, 4))
    return (
        ends,
        mine[:2][None],
        mine[2:][None],
        jnp.stack([gq, gk, gv], 1)[None],
        head_grads[None],
        go.transpose(1, 2, 0)[None],
        grads[48:96].T[None],
        up_row[None],
        grads[96:][None],
    )


def solution(mesh):
    placed = (
        P("pipe", None, ("fsdp", "tp"), None),
        P(None, "fsdp"),
        P("pipe", None, ("fsdp", "tp")),
        P("pipe", None, ("fsdp", "tp")),
        P("pipe", "fsdp", None, "tp", None),
        P("pipe", None, "tp", "fsdp"),
        P("pipe", "tp", None, "fsdp"),
        P("pipe", None, ("fsdp", "tp")),
        P("pipe", ("fsdp", "tp")),
        P("pipe", ("fsdp", "tp"), None),
    )
    return jax.shard_map(
        on_device,
        mesh=mesh,
        in_specs=placed,
        out_specs=(placed[0], *placed[2:]),
        check_vma=False,
    )
```

time: 2150 us -> 264 us (0.12)
  blocking collectives: 1100 us -> 0 us
  waiting for transfers between devices: 578 us -> 0 us
  Pallas kernels: 0 us -> 244 us
  local copies, waits for them, and re-layouts: 179 us -> 13.4 us
  matrix products: 157 us -> 0 us
  other arithmetic: 66.6 us -> 5.05 us
  starting transfers between devices: 41.2 us -> 0 us
    unnamed x12 -> x0, blocking collectives: 675 us -> none
    all_gather x5 -> x0, blocking collectives: 420 us -> none  [the longest x1 180 us: fetch(): lax.all_gather(vector_shards[1], ('fsdp', 'tp'), axis=1, tiled=True)]
    reduce_scatter x12 -> x0, waiting for transfers between devices: 376 us -> none  [the longest x3 228 us: on_device(): lax.psum_scatter(matrix_grads[0].astype(jnp.bfloat16), 'fsdp', scatter_di...]
    pallas_call x0 -> x1, Pallas kernels: none -> 244 us  [on_device(): pl.pallas_call(layer_kernel, out_shape=(jax.ShapeDtypeStruct((ROWS, 768),...]
    all_gather x14 -> x0, waiting for transfers between devices: 186 us -> none  [the longest x6 71.3 us: spread_grads(): return lax.all_gather(values, 'tp', axis=0, tiled=True)]
    dot_general x52 -> x0, matrix products: 150 us -> none  [the longest x3 29.9 us: forward(): jnp.dot(full_two, up_proj, preferred_element_type=jnp.float32)]
    unnamed x300 -> x19, local copies, waits for them, and re-layouts: 93.9 us -> 3.53 us
    unnamed x12 -> x0, starting transfers between devices: 33 us -> none
  transfers between devices with their start and end apart: 42 -> 0, of which waited for: 25 -> 0; matrix products, arithmetic and copies ran while one was open for 12% -> 0% of each run, Pallas kernels for 0% -> 0%
where the time goes in v1:
time: 264 us; the launch traced here: 263 us
  Pallas kernels  244 us (92%)
  local copies, waits for them, and re-layouts  13.4 us (5%)
  other arithmetic  5.05 us (2%)
    pallas_call x1, Pallas kernels, on_device(): pl.pallas_call(layer_kernel, out_shape=(jax.ShapeDtypeStruct((ROWS, 768),...  244 us

profile of v1, /device:TPU:0, one launch (start us, length us, event | category | flops | bytes accessed | tf_op | source)
XLA Modules:
  0.0 263.1 jit_solution(2620182718845135973)
XLA Ops:
  0.6 0.0 copy-start.1
  0.7 0.9 slice_bitcast_fusion.2
  1.5 0.7 slice_bitcast_fusion.17
  2.3 0.0 copy-start.2
  2.3 0.0 copy-start.3
  2.3 0.1 concatenate.26
  2.4 0.7 copy-done.2
  3.2 0.0 copy-done.3
  3.2 0.7 pad_maximum_fusion.w_hbm
  3.9 0.0 copy-start.6
  3.9 0.7 copy-done.6
  4.6 0.0 copy-done.1
  4.6 0.6 broadcast_select_fusion.1
  5.2 0.1 copy.27
  5.2 0.9 pad.4.clone
  6.1 0.0 copy-start.8
  6.1 0.7 copy-done.8
  6.8 0.1 tile.39
  6.9 0.0 copy-start.4
  6.9 0.7 copy-done.4
  7.5 0.1 tile.42
  7.7 0.1 concatenate.32
  7.8 0.1 fusion.2
  7.9 0.0 copy-start.5
  7.9 0.0 copy-start.7
  7.9 0.7 copy-done.5
  8.5 0.0 copy-done.7
  8.6 0.1 tile.35
  8.8 0.1 pad.31.clone
  8.8 0.7 maximum_maximum_fusion.vec_hbm
  9.5 243.9 %shard_map.169 = (bf16[416,768]{1,0:T(8,128)(2,1)}, f32[144,768]{1,0:T(8,128)}, f32[16,768]{1,0:T(8,128)}) custom-call(bf16[3,48,768]{2,1,0:T(8,128)(2,1)} %pad_maximum_fusion.w_hbm, bf16[416,768]{1,0:T(8,128)(2,1)} %bitcast.127, f32[16,768]{1,0:T(8,128)} %maximum_maximum_fusion.vec_hbm), custom_call_target="tpu_custom_call" | custom-call | tf_op jit(solution)/shard_map/pallas_call | solution.py:594
  253.4 1.1 slice.234
  254.5 0.0 copy-start
  254.6 1.5 fusion
  256.0 0.8 constant_dynamic-slice_fusion.1
  256.8 0.6 slice_bitcast_fusion.30
  257.4 0.6 slice_bitcast_fusion.29
  257.9 0.0 copy-done
  257.9 0.1 slice_bitcast_fusion.7
  258.1 0.7 maximum_bitcast_fusion
  258.8 0.8 constant_dynamic-slice_fusion
  259.7 0.1 dynamic-slice_maximum_fusion
  259.8 0.6 copy.32
  260.3 0.6 maximum_bitcast_fusion.4
  261.0 0.7 slice_bitcast_fusion
  261.7 0.8 slice.211
  262.5 0.6 dynamic-slice_bitcast_fusion
  (23 shorter events, 0.2 us)
Async XLA Ops:
  0.6 3.9 %copy-start.1 = (bf16[1,2,197,768]{3,1,2,0:T(2,128)(2,1)S(1)}, bf16[1,2,197,768]{3,1,2,0:T(2,128)(2,1)}, u32[]{:S(2)}) copy-start(bf16[1,2,197,768]{3,1,2,0:T(2,128)(2,1)} %param.10) | copy-start | bytes 1815556
  2.3 0.9 copy-start.2
  2.3 0.9 copy-start.3
  3.9 0.7 copy-start.6
  6.1 0.7 copy-start.8
  6.9 0.7 copy-start.4
  7.9 0.7 copy-start.5
  7.9 0.7 copy-start.7
  254.5 3.4 %copy-start = (f32[144,768]{1,0:T(8,128)S(1)}, f32[144,768]{1,0:T(8,128)}, u32[]{:S(2)}) copy-start(f32[144,768]{1,0:T(8,128)} %get-tuple-element.14) | copy-start | bytes 1327108

commit v2 on v1

--- a/solution.py
+++ b/solution.py
@@ -178,9 +178,10 @@
     def finish(self, phase):
         for which in range(3):
             self.copy(phase, which).wait_recv()
-        self.stages[phase + 1] = (self.stages[phase] + self.landings[phase, 0]) + (
-            self.landings[phase, 1] + self.landings[phase, 2]
-        )
+        total = self.stages[phase].astype(f32)
+        for which in range(3):
+            total = total + self.landings[phase, which].astype(f32)
+        self.stages[phase + 1] = total.astype(self.stages.dtype)
 
     def drain(self):
         for phase in range(3):
@@ -200,6 +201,7 @@
 
 SEQ, IMG, ROWS = 197, 208, 416
 CHUNK = 32
+UNROLL = 13
 EPS = 1e-6
 
 
@@ -234,46 +236,48 @@
 def row_loop(body, init=None):
     def step(i, carry):
         return body(pl.ds(pl.multiple_of(i * CHUNK, CHUNK), CHUNK), carry)
-    return lax.fori_loop(0, ROWS // CHUNK, step, init)
+    return lax.fori_loop(0, ROWS // CHUNK, step, init, unroll=UNROLL)
 
 
 def square(ref, kind, j, lo=0, hi=768):
     return ref[kind, j, :, :, :, lo:hi].reshape(768, hi - lo)
 
 
-def forward(r):
+def forward_attention(r, hook=None):
     vec = r.vec
 
     def first_norm(rows, _):
         xhat, _inv = normed(r.x[rows, :].astype(f32))
-        r.n1[rows, :] = (xhat * vec[0:1, :] + vec[2:3, :]).astype(bf16)
+        r.n1[rows, :] = (xhat * vec[8:9, :] + vec[9:10, :]).astype(bf16)
     row_loop(first_norm)
 
     low = lax.broadcasted_iota(jnp.int32, (IMG, 128), 1) < 64
-    keyed = lax.broadcasted_iota(jnp.int32, (IMG, IMG), 1) < SEQ
+    keyed = lax.broadcasted_iota(jnp.int32, (IMG, IMG), 0) < SEQ
     zero = jnp.zeros((IMG, 128), bf16)
 
     def head_group(t, _):
         r.q[t] = (nn(r.n1[...], square(r.w, 0, t, 0, 640)) + vec[pl.ds(10 + t, 1), 0:640]).astype(bf16)
 
-        def image(i, _):
-            rows = pl.ds(pl.multiple_of(i * IMG, IMG), IMG)
+        def image(i):
+            rows = slice(i * IMG, (i + 1) * IMG)
             tq, tk, tv, t3, t4 = (r.q[t, rows, k * 128:(k + 1) * 128] for k in range(5))
 
             def probs(h, qs, ks):
-                s = nt(qs, ks) * 0.125
-                s = jnp.where(keyed, s, -1e30)
-                e = jnp.exp(s - jnp.max(s, -1, keepdims=True))
-                p = (e * (1.0 / jnp.sum(e, -1, keepdims=True))).astype(bf16)
+                s = jnp.where(keyed, nt(ks, qs) * 0.125, -1e30)
+                e = jnp.exp(s - jnp.max(s, 0, keepdims=True))
+                p = (e * (1.0 / jnp.sum(e, 0, keepdims=True))).astype(bf16)
                 r.p[(t * 2 + i) * 3 + h] = p
                 return p
             p0 = probs(0, jnp.where(low, tq, zero), tk)
             p1 = probs(1, jnp.where(low, zero, tq), tk)
             p2 = probs(2, jnp.where(low, t3, zero), t4)
-            r.mx[t, rows, 0:128] = jnp.where(low, 0.0, nn(p2, t3)).astype(bf16)
-            r.mx[t, rows, 128:256] = jnp.where(low, nn(p0, tv), nn(p1, tv)).astype(bf16)
-            return 0
-        lax.fori_loop(0, 2, image, 0)
+            tvt = tv.T
+            o01 = jnp.concatenate([nn(tvt[0:64], p0), nn(tvt[64:128], p1)], 0).astype(bf16)
+            o2 = jnp.concatenate([jnp.zeros((64, IMG), bf16), nn(t3.T[64:128], p2).astype(bf16)], 0)
+            r.mx[t, rows, 0:128] = o2.T
+            r.mx[t, rows, 128:256] = o01.T
+        image(0)
+        image(1)
         part = nt(r.mx[t], square(r.w, 0, t, 512, 768))
 
         @pl.when(t == 0)
@@ -283,47 +287,48 @@
         @pl.when(t > 0)
         def _():
             r.acc[...] += part
+        if hook is not None:
+            hook(t)
         return 0
     lax.fori_loop(0, 4, head_group, 0)
 
+
+def forward_ffn(r):
+    vec = r.vec
+
     def second_norm(rows, _):
-        h1 = r.x[rows, :].astype(f32) + r.acc[rows, :] + vec[3:4, :]
+        h1 = r.x[rows, :].astype(f32) + r.acc[rows, :] + vec[1:2, :]
         r.h1[rows, :] = h1
         xhat, _inv = normed(h1)
-        r.n2[rows, :] = (xhat * vec[1:2, :] + vec[4:5, :]).astype(bf16)
-        r.acc[rows, :] = h1 + vec[5:6, :]
+        r.n2[rows, :] = (xhat * vec[0:1, :] + vec[2:3, :]).astype(bf16)
+        r.acc[rows, :] = h1 + vec[3:4, :]
     row_loop(second_norm)
 
     def hidden(j, _):
-        r.tmp[...] = nt(r.n2[...], square(r.w, 1, j)) + vec[pl.ds(6 + j, 1), :]
-
-        def gelu(rows, _):
-            u = r.tmp[rows, :]
+        up = square(r.w, 1, j)
+        for c in range(3):
+            cols = slice(c * 256, (c + 1) * 256)
+            u = nt(r.n2[...], up[cols]) + vec[pl.ds(4 + j, 1), cols]
             cdf = 0.5 * (1.0 + lax.erf(u * 0.7071067811865476))
-            r.act[j, rows, :] = (u * cdf).astype(bf16)
-            r.gp[j, rows, :] = (cdf + u * (jnp.exp(-0.5 * u * u) * 0.3989422804014327)).astype(bf16)
-        row_loop(gelu)
+            r.act[j, :, cols] = (u * cdf).astype(bf16)
+            r.gp[j, :, cols] = (cdf + u * (jnp.exp(-0.5 * u * u) * 0.3989422804014327)).astype(bf16)
         r.acc[...] += nn(r.act[j], square(r.w, 2, j))
         return 0
     lax.fori_loop(0, 4, hidden, 0)
 
 
-def backward_ffn(r):
+def backward_ffn(r, hook=None):
     vec = r.vec
     dvec = r.dvec
 
     def hidden(j, _):
-        r.tmp[...] = nt(r.gy[...], square(r.w, 2, j))
-
-        def chain(rows, total):
-            du = (r.tmp[rows, :] * r.gp[j, rows, :].astype(f32)).astype(bf16)
-            r.dx[rows, :] = du
-            return total + fold(du.astype(f32))
-        total = row_loop(chain, jnp.zeros((8, 768), f32))
-        dvec[pl.ds(6 + j, 1), :] = jnp.sum(total, 0, keepdims=True)
-        r.g[2, j] = tn(r.act[j], r.gy[...]).astype(bf16).reshape(4, 4, 48, 768)
-        r.g[1, j] = tn(r.dx[...], r.n2[...]).astype(bf16).reshape(4, 4, 48, 768)
-        part = nn(r.dx[...], square(r.w, 1, j))
+        down = square(r.w, 2, j)
+        for c in range(3):
+            cols = slice(c * 256, (c + 1) * 256)
+            du = (nt(r.gy[...], down[cols]) * r.gp[j, :, cols].astype(f32)).astype(bf16)
+            r.gp[j, :, cols] = du
+            dvec[pl.ds(4 + j, 1), cols] = jnp.sum(du.astype(f32), 0, keepdims=True)
+        part = nn(r.gp[j], square(r.w, 1, j))
 
         @pl.when(j == 0)
         def _():
@@ -332,6 +337,8 @@
         @pl.when(j > 0)
         def _():
             r.acc[...] += part
+        if hook is not None:
+            hook(j)
         return 0
     lax.fori_loop(0, 4, hidden, 0)
 
@@ -339,77 +346,104 @@
         dn = r.acc[rows, :]
         gy = r.gy[rows, :].astype(f32)
         xhat, inv = normed(r.h1[rows, :])
-        dh = gy + norm_back(dn, xhat, inv, vec[1:2, :])
-        r.tmp[rows, :] = dh
+        dh = gy + norm_back(dn, xhat, inv, vec[0:1, :])
+        r.h1[rows, :] = dh
         gh = dh.astype(bf16)
-        r.n2[rows, :] = gh
+        r.gh[rows, :] = gh
         return (sums[0] + fold(dn * xhat), sums[1] + fold(dn), sums[2] + fold(gh.astype(f32)), sums[3] + fold(gy))
     zero = jnp.zeros((8, 768), f32)
     sums = row_loop(norm_two, (zero,) * 4)
-    for row, total in zip((1, 4, 3, 5), sums):
+    for row, total in zip((0, 2, 1, 3), sums):
         dvec[row:row + 1, :] = jnp.sum(total, 0, keepdims=True)
 
 
-def backward_attention(r):
-    vec = r.vec
+def grads_down(r):
+    def hidden(j, _):
+        r.g[2, j] = tn(r.act[j], r.gy[...]).astype(bf16).reshape(4, 4, 48, 768)
+        return 0
+    lax.fori_loop(0, 4, hidden, 0)
+
+
+def grads_up(r):
+    def hidden(j, _):
+        r.g[1, j] = tn(r.gp[j], r.n2[...]).astype(bf16).reshape(4, 4, 48, 768)
+        return 0
+    lax.fori_loop(0, 4, hidden, 0)
+
+
+def backward_attention(r, hook=None):
     dvec = r.dvec
-    dqkv, dmixed = r.gp.at[0], r.gp.at[1]
     low = lax.broadcasted_iota(jnp.int32, (IMG, 128), 1) < 64
     zero = jnp.zeros((IMG, 128), bf16)
 
     def head_group(t, _):
-        dmixed[:, 0:256] = nn(r.n2[...], square(r.w, 0, t, 512, 768)).astype(bf16)
-
-        def image(i, _):
-            rows = pl.ds(pl.multiple_of(i * IMG, IMG), IMG)
+        r.dm[...] = nn(r.gh[...], square(r.w, 0, t, 512, 768)).astype(bf16)
+
+        def image(i):
+            rows = slice(i * IMG, (i + 1) * IMG)
             tq, tk, tv, t3, t4 = (r.q[t, rows, k * 128:(k + 1) * 128] for k in range(5))
-            d4 = dmixed[rows, 0:128]
-            d5 = dmixed[rows, 128:256]
-
-            def head(h, d_full, d_masked, v, q, k):
+            d4 = r.dm[rows, 0:128]
+            d5 = r.dm[rows, 128:256]
+
+            def head(h, d_full, d_masked, v, q, kt):
                 p = r.p[(t * 2 + i) * 3 + h]
                 pf = p.astype(f32)
-                dv = tn(p, d_full)
-                dp = nt(d_masked, v)
-                ds = (pf * (dp - jnp.sum(dp * pf, -1, keepdims=True))).astype(bf16)
-                return nn(ds, k) * 0.125, tn(ds, q) * 0.125, dv
-            dq0, dk0, dv0 = head(0, d5, jnp.where(low, d5, zero), tv, tq, tk)
-            dq1, dk1, dv1 = head(1, d5, jnp.where(low, zero, d5), tv, tq, tk)
-            dqkv[rows, 0:128] = jnp.where(low, dq0, dq1).astype(bf16)
-            dqkv[rows, 128:256] = jnp.where(low, dk0, dk1).astype(bf16)
-            dqkv[rows, 256:384] = jnp.where(low, dv0, dv1).astype(bf16)
-            dq2, dk2, dv2 = head(2, d4, jnp.where(low, zero, d4), t3, t3, t4)
-            dqkv[rows, 384:512] = jnp.where(low, dq2, dv2).astype(bf16)
-            dqkv[rows, 512:640] = jnp.where(low, dk2, 0.0).astype(bf16)
-            return 0
-        lax.fori_loop(0, 2, image, 0)
-        dvec[pl.ds(10 + t, 1), 0:640] = jnp.sum(dqkv[:, 0:640].astype(f32), 0, keepdims=True)
-        ga = tn(r.n1[...], dqkv[:, 0:640])
-        go = tn(r.n2[...], r.mx[t])
+                dv = nn(p, d_full)
+                dp = nt(v, d_masked)
+                ds = (pf * (dp - jnp.sum(dp * pf, 0, keepdims=True))).astype(bf16)
+                return nn(kt, ds), nn(ds, q) * 0.125, dv
+            tkt = tk.T
+            dq0, dk0, dv0 = head(0, d5, jnp.where(low, d5, zero), tv, tq, tkt[0:64])
+            dq1, dk1, dv1 = head(1, d5, jnp.where(low, zero, d5), tv, tq, tkt[64:128])
+            dq2, dk2, dv2 = head(2, d4, jnp.where(low, zero, d4), t3, t3, t4.T[0:64])
+            r.q[t, rows, 0:128] = (jnp.concatenate([dq0, dq1], 0) * 0.125).astype(bf16).T
+            r.q[t, rows, 128:256] = jnp.where(low, dk0, dk1).astype(bf16)
+            r.q[t, rows, 256:384] = jnp.where(low, dv0, dv1).astype(bf16)
+            dq2 = jnp.concatenate([(dq2 * 0.125).astype(bf16), jnp.zeros((64, IMG), bf16)], 0).T
+            r.q[t, rows, 384:512] = jnp.where(low, dq2, dv2.astype(bf16))
+            r.q[t, rows, 512:640] = jnp.where(low, dk2, 0.0).astype(bf16)
+        image(0)
+        image(1)
+        dvec[pl.ds(10 + t, 1), 0:640] = jnp.sum(r.q[t].astype(f32), 0, keepdims=True)
+        part = nt(r.q[t], square(r.w, 0, t, 0, 640))
+
+        @pl.when(t == 0)
+        def _():
+            r.acc[...] = part
+
+        @pl.when(t > 0)
+        def _():
+            r.acc[...] += part
+        if hook is not None:
+            hook(t)
+        return 0
+    lax.fori_loop(0, 4, head_group, 0)
+
+
+def grads_attention(r):
+    def head_group(t, _):
+        ga = tn(r.n1[...], r.q[t])
+        go = tn(r.gh[...], r.mx[t])
         r.g[0, t, :, :, :, 0:512] = ga[:, 0:512].astype(bf16).reshape(4, 4, 48, 512)
         r.g[0, t, :, :, :, 512:640] = (ga[:, 512:640] + go[:, 0:128]).astype(bf16).reshape(4, 4, 48, 128)
         r.g[0, t, :, :, :, 640:768] = go[:, 128:256].astype(bf16).reshape(4, 4, 48, 128)
-        part = nt(dqkv[:, 0:640], square(r.w, 0, t, 0, 640))
-
-        @pl.when(t == 0)
-        def _():
-            r.acc[...] = part
-
-        @pl.when(t > 0)
-        def _():
-            r.acc[...] += part
         return 0
     lax.fori_loop(0, 4, head_group, 0)
+
+
+def backward_end(r):
+    vec = r.vec
+    dvec = r.dvec
 
     def norm_one(rows, sums):
         dn = r.acc[rows, :]
         xhat, inv = normed(r.x[rows, :].astype(f32))
-        dx = r.tmp[rows, :] + norm_back(dn, xhat, inv, vec[0:1, :])
+        dx = r.h1[rows, :] + norm_back(dn, xhat, inv, vec[8:9, :])
         r.dx[rows, :] = dx.astype(bf16)
         return (sums[0] + fold(dn * xhat), sums[1] + fold(dn))
     zero = jnp.zeros((8, 768), f32)
     sums = row_loop(norm_one, (zero,) * 2)
-    for row, total in zip((0, 2), sums):
+    for row, total in zip((8, 9), sums):
         dvec[row:row + 1, :] = jnp.sum(total, 0, keepdims=True)
 
 
@@ -418,9 +452,8 @@
     x=pltpu.VMEM((ROWS, 768), bf16), n1=pltpu.VMEM((ROWS, 768), bf16), q=pltpu.VMEM((4, ROWS, 640), bf16),
     p=pltpu.VMEM((24, IMG, IMG), bf16), mx=pltpu.VMEM((4, ROWS, 256), bf16), acc=pltpu.VMEM((ROWS, 768), f32),
     h1=pltpu.VMEM((ROWS, 768), f32), n2=pltpu.VMEM((ROWS, 768), bf16), act=pltpu.VMEM((4, ROWS, 768), bf16),
-    gp=pltpu.VMEM((4, ROWS, 768), bf16), tmp=pltpu.VMEM((ROWS, 768), f32), gy=pltpu.VMEM((ROWS, 768), bf16),
-
-    dx=pltpu.VMEM((ROWS, 768), bf16),
+    gp=pltpu.VMEM((4, ROWS, 768), bf16), gy=pltpu.VMEM((ROWS, 768), bf16), gh=pltpu.VMEM((ROWS, 768), bf16),
+    dm=pltpu.VMEM((ROWS, 256), bf16), dx=pltpu.VMEM((ROWS, 768), bf16),
     vec=pltpu.VMEM((16, 768), f32), dvec=pltpu.VMEM((16, 768), f32),
     w=pltpu.VMEM(SLOTS, bf16), g=pltpu.VMEM(SLOTS, bf16),
 )
@@ -432,8 +465,9 @@
 def layer_kernel(w_hbm, rows_hbm, vec_hbm, end_hbm, grad_hbm, dvec_hbm, *scratch):
     r = types.SimpleNamespace(**dict(zip(NAMES, scratch)))
     rest = scratch[len(NAMES) :]
-    landings, out = rest[:6], r.acc
-    stages, sum_landings, ag_send, ag_recv, rs_send, rs_recv, sum_send, sum_recv, link, local = rest[6:]
+    landings, out = rest[:6], r.h1
+    stages, sum_landings = rest[6:9], rest[9:12]
+    ag_send, ag_recv, rs_send, rs_recv, sum_send, sum_recv, link, local, ready = rest[12:]
     coords = place()
     first = lax.axis_index("pipe") == 0
     second = lax.axis_index("pipe") == 1
@@ -447,7 +481,7 @@
     ]
     for copy in own:
         copy.start()
-    vec_in = pltpu.make_async_copy(vec_hbm, stages.at[0, 0], local.at[3])
+    vec_in = pltpu.make_async_copy(vec_hbm, stages[0].at[0], local.at[3])
     vec_in.start()
 
     @pl.when(first)
@@ -467,21 +501,51 @@
     vec_in.wait()
 
     gathers = [Gather(r.w, kind, third, coords, ag_send, ag_recv) for kind in range(3) for third in range(3)]
-    sums = [
-        AllSum(stages.at[k], sum_landings.at[k], coords, sum_send.at[k], sum_recv.at[k]) for k in range(2)
-    ]
-    for number in range(9):
-        for gather in gathers:
-            gather.step(number)
-        if number % 3 == 0:
-            sums[0].start(number // 3)
-        elif number % 3 == 1:
-            sums[0].finish(number // 3)
-    r.vec[...] = stages[0, 3]
+    sums = [AllSum(stages[k], sum_landings[k], coords, sum_send.at[k], sum_recv.at[k]) for k in range(3)]
+
+    def each(movers, *numbers):
+        for number in numbers:
+            for mover in movers:
+                mover.step(number)
+
+    early, late = gathers[:3], gathers[3:]
+    sums[0].start(0)
+    each(early, 0)
+    each(late, 0)
+    sums[0].finish(0)
+    sums[0].start(1)
+    each(early, 1)
+    each(late, 1)
+    each(early, 2, 3)
+    sums[0].finish(1)
+    sums[0].start(2)
+    each(late, 2, 3)
+    each(early, 4)
+    sums[0].finish(2)
+    each(late, 4)
+    each(early, 5)
+
+    @pl.when(second)
+    def _():
+        each(late, 5)
+        pl.semaphore_wait(ready, 1)
+
+    each(early, 6)
+
+    @pl.when(first)
+    def _():
+        each(late, 5)
+
+    each(late, 6)
+    each(early, 7, 8)
+
+    @pl.when(first)
+    def _():
+        pl.semaphore_signal(ready, inc=1, device_id=sibling(), device_id_type=MESH)
+        each(late, 7)
+
+    r.vec[...] = stages[0][3].astype(f32)
     r.dvec[...] = jnp.zeros_like(r.dvec)
-    for gather in gathers:
-        gather.drain()
-    sums[0].drain()
 
     up = pltpu.make_async_remote_copy(
         src_ref=r.dx, dst_ref=r.x, send_sem=link.at[0], recv_sem=link.at[1], device_id=sibling(), device_id_type=MESH
@@ -493,60 +557,118 @@
 
     @pl.when(second)
     def _():
+        each(late, 7)
         up.wait_recv()
 
-    forward(r)
+    forward_attention(r)
+    each(late, 8)
+    forward_ffn(r)
     r.dx[...] = r.acc[...].astype(bf16)
 
     @pl.when(first)
     def _():
         up.start()
+
+    @pl.when(second)
+    def _():
+        end.start()
+
+    for gather in gathers:
+        gather.drain()
+    sums[0].drain()
+
+    @pl.when(first)
+    def _():
         up.wait_send()
         down.wait_recv()
 
-    @pl.when(second)
-    def _():
-        end.start()
-        end.wait()
-
-    backward_ffn(r)
     scatters = [
         Scatter(r.g, kind, third, coords, landings, rs_send, rs_recv, out) for kind in range(3) for third in range(3)
     ]
-    for scatter in scatters[3:]:
-        scatter.step(0)
-    backward_attention(r)
+    sa, su, sd = scatters[:3], scatters[3:6], scatters[6:]
+    grads_down(r)
+    each(sd, 0)
+
+    def during_ffn(j):
+        @pl.when(j == 2)
+        def _():
+            each(sd, 1)
+
+    backward_ffn(r, during_ffn)
+    stages[1][0] = r.dvec[0:8, :]
+    sums[1].start(0)
+    grads_up(r)
+    each(su, 0)
+    def during_attention(t):
+        @pl.when(t == 3)
+        def _():
+            sums[1].finish(0)
+            sums[1].start(1)
+            each(sd, 2, 3)
+            each(su, 1)
+
+    backward_attention(r, during_attention)
+
+    @pl.when(second)
+    def _():
+        end.wait()
+
+    backward_end(r)
 
     @pl.when(first)
     def _():
         end.start()
-        end.wait()
 
     @pl.when(second)
     def _():
         down.start()
-        down.wait_send()
-
-    stages[1, 0] = r.dvec[...]
-    for scatter in scatters[:3]:
-        scatter.step(0)
-    for number in range(9):
-        for scatter in scatters:
-            if number:
-                scatter.step(number)
-        if number % 3 == 0:
-            sums[1].start(number // 3)
-        elif number % 3 == 1:
-            sums[1].finish(number // 3)
-    for scatter in scatters:
-        scatter.drain()
-    sums[1].drain()
+
+    stages[2][0] = r.dvec[8:16, :]
+    sums[2].start(0)
+    grads_attention(r)
+    sums[2].finish(0)
+    sums[2].start(1)
+    each(sa, 0)
+    sums[1].finish(1)
+    sums[1].start(2)
+    each(sd, 4)
+    each(su, 2, 3)
+    sums[2].finish(1)
+    sums[2].start(2)
+    each(sa, 1)
+    each(sd, 5, 6)
+    each(su, 4)
+    sums[1].finish(2)
+    each(sa, 2, 3)
+    each(sd, 7)
+    each(su, 5, 6)
+    sums[2].finish(2)
+    each(sa, 4)
+    each(sd, 8)
+    each(su, 7)
+    each(sa, 5, 6)
+    each(su, 8)
+    each(sa, 7, 8)
     copies = [
         pltpu.make_async_copy(out.at[pl.ds(0, 144)], grad_hbm, local.at[0]),
-        pltpu.make_async_copy(stages.at[1, 3], dvec_hbm, local.at[1]),
+        pltpu.make_async_copy(stages[1].at[3], dvec_hbm.at[pl.ds(0, 8)], local.at[1]),
+        pltpu.make_async_copy(stages[2].at[3], dvec_hbm.at[pl.ds(8, 8)], local.at[2]),
     ]
     for copy in copies:
         copy.start()
+    for scatter in scatters:
+        scatter.drain()
+    for some in sums[1:]:
+        some.drain()
+
+    @pl.when(first)
+    def _():
+        end.wait()
+
+    @pl.when(second)
+    def _():
+        down.wait_send()
+
     for copy in copies:
         copy.wait()
 
@@ -577,17 +699,18 @@
     weights = jnp.stack([units(wq[:, 0], wq[:, 1], wq[:, 2], wo), w_up[0].T, w_down[0]], 0)
 
     lanes = jnp.arange(768, dtype=jnp.int32)
-    small = jnp.concatenate([norm_gains[0], row_biases[0]], 0).astype(f32)
-    small = jnp.where(lanes // 12 == chip, jnp.tile(small, (1, 64)), 0.0)
+    gains, biases = norm_gains[0], row_biases[0]
+    small = jnp.concatenate([gains[1:], biases[1:], gains[:1], biases[:1]], 0)
+    small = jnp.where(lanes // 12 == chip, jnp.tile(small, (1, 64)), 0)
     hidden = jnp.arange(3072, dtype=jnp.int32)
-    hidden = jnp.where(hidden // 48 == chip, jnp.tile(up_bias[0].astype(f32), 64), 0.0).reshape(4, 768)
+    hidden = jnp.where(hidden // 48 == chip, jnp.tile(up_bias[0], 64), 0).reshape(4, 768)
     heads = jnp.where(
-        jnp.arange(64, dtype=jnp.int32) // 4 == fsdp, jnp.tile(qv_bias[0].astype(f32), (1, 1, 16)), 0.0
+        jnp.arange(64, dtype=jnp.int32) // 4 == fsdp, jnp.tile(qv_bias[0], (1, 1, 16)), 0
     )
     none = jnp.zeros_like(heads[0])
     heads = units(heads[0], none, heads[1], none)
-    heads = jnp.where(jnp.arange(4, dtype=jnp.int32)[:, None] == tp, heads[None], 0.0)
-    vec = jnp.concatenate([small, hidden, heads, jnp.zeros((2, 768), f32)], 0)
+    heads = jnp.where(jnp.arange(4, dtype=jnp.int32)[:, None] == tp, heads[None], 0)
+    vec = jnp.concatenate([small[:4], hidden, small[4:], heads, jnp.zeros((2, 768), bf16)], 0)
 
     anywhere = pl.BlockSpec(memory_space=pl.ANY)
     dma = pltpu.SemaphoreType.DMA
@@ -603,16 +726,21 @@
         scratch_shapes=[
             *BODY_SCRATCH.values(),
             *LANDINGS,
-            pltpu.VMEM((2, 4, 16, 768), f32),
-            pltpu.VMEM((2, 3, 3, 16, 768), f32),
+            pltpu.VMEM((4, 16, 768), bf16),
+            pltpu.VMEM((4, 8, 768), f32),
+            pltpu.VMEM((4, 8, 768), f32),
+            pltpu.VMEM((3, 3, 16, 768), bf16),
+            pltpu.VMEM((3, 3, 8, 768), f32),
+            pltpu.VMEM((3, 3, 8, 768), f32),
             dma((9, 3, 4)),
             dma((9, 3, 4)),
             dma((9, 3, 4)),
             dma((9, 3, 4)),
-            dma((2, 3, 3)),
-            dma((2, 3, 3)),
+            dma((3, 3, 3)),
+            dma((3, 3, 3)),
             dma((4,)),
             dma((6,)),
+            pltpu.SemaphoreType.REGULAR,
         ],
         compiler_params=pltpu.CompilerParams(
             collective_id=0, has_side_effects=True, vmem_limit_bytes=63 * 2**20
@@ -622,15 +750,15 @@
     end = end.reshape(2, IMG, 768)[:, :SEQ]
     ends = jnp.where(first | live, end, 0)[None]
     gq, gk, gv, go = split_units(grads[:48])
-    mine = lax.dynamic_slice(dvec, (0, chip * 12), (6, 12))
-    up_row = lax.dynamic_slice(dvec[6:10].reshape(3072), (chip * 48,), (48,))
+    mine = lax.dynamic_slice(dvec, (0, chip * 12), (10, 12))
+    up_row = lax.dynamic_slice(dvec[4:8].reshape(3072), (chip * 48,), (48,))
     head_row = lax.dynamic_slice(dvec, (10 + tp, 0), (1, 640))[0]
     hq, _, hv, _ = split_units(head_row)
     head_grads = lax.dynamic_slice(jnp.stack([hq, hv], 0), (0, 0, fsdp * 4), (2, 3, 4))
     return (
         ends,
-        mine[:2][None],
-        mine[2:][None],
+        jnp.stack([mine[8], mine[0]], 0)[None],
+        jnp.stack([mine[9], mine[1], mine[2], mine[3]], 0)[None],
         jnp.stack([gq, gk, gv], 1)[None],
         head_grads[None],
         go.transpose(1, 2, 0)[None],

time: 264 us -> 204 us (0.77)
  Pallas kernels: 244 us -> 183 us
    pallas_call x1, Pallas kernels: 244 us -> 183 us  [on_device(): pl.pallas_call(layer_kernel, out_shape=(jax.ShapeDtypeStruct((ROWS, 768),...]
where the time goes in v2:
time: 204 us
  Pallas kernels  183 us (90%)
  local copies, waits for them, and re-layouts  14.2 us (7%)
  other arithmetic  5.52 us (3%)
    pallas_call x1, Pallas kernels, on_device(): pl.pallas_call(layer_kernel, out_shape=(jax.ShapeDtypeStruct((ROWS, 768),...  183 us

profile of v2, /device:TPU:0, one launch (start us, length us, event | category | flops | bytes accessed | tf_op | source)
XLA Modules:
  0.0 203.5 jit_solution(3217233387024074699)
XLA Ops:
  0.6 0.0 copy-start.1
  0.7 0.9 slice_bitcast_fusion.2
  1.5 0.7 slice_bitcast_fusion.17
  2.3 0.0 copy-start.2
  2.3 0.0 copy-start.3
  2.3 0.1 concatenate.18
  2.4 0.7 copy-done.2
  3.2 0.0 copy-done.3
  3.2 0.7 pad_maximum_fusion.w_hbm
  3.9 0.0 copy-start.8
  3.9 0.7 copy-done.8
  4.6 0.0 copy-done.1
  4.6 0.6 broadcast_select_fusion.1
  5.2 0.1 copy.27
  5.2 0.9 pad.4.clone
  6.1 0.0 copy-start.4
  6.1 0.0 copy-start.5
  6.1 0.7 copy-done.4
  6.8 0.0 copy-done.5
  6.8 0.2 tile.32
  7.1 0.0 copy-start.7
  7.1 0.6 copy-done.7
  7.7 0.1 tile.35
  7.8 0.0 copy-start.6
  7.8 0.7 copy-done.6
  8.5 0.1 tile.39
  8.7 0.1 concatenate.22
  8.8 0.1 fusion.3
  8.9 1.3 concatenate.23.vec_hbm
  10.1 182.9 %shard_map.169 = (bf16[416,768]{1,0:T(8,128)(2,1)}, f32[144,768]{1,0:T(8,128)}, f32[16,768]{1,0:T(8,128)}) custom-call(bf16[3,48,768]{2,1,0:T(8,128)(2,1)} %pad_maximum_fusion.w_hbm, bf16[416,768]{1,0:T(8,128)(2,1)} %bitcast.129, bf16[16,768]{1,0:T(8,128)(2,1)} %concatenate.23.vec_hbm), custom_call_target="tpu_custom_call" | custom-call | tf_op jit(solution)/shard_map/pallas_call | solution.py:717
  193.1 1.1 slice.287
  194.2 0.0 copy-start
  194.2 1.5 fusion
  195.7 0.8 fusion.9
  196.5 0.6 maximum_bitcast_fusion.8
  197.1 0.8 dynamic-slice.3
  197.8 0.6 maximum_bitcast_fusion.5
  198.4 0.0 copy-done
  198.4 0.1 slice_bitcast_fusion.7
  198.6 0.7 maximum_bitcast_fusion
  199.3 0.8 constant_dynamic-slice_fusion
  200.2 0.1 dynamic-slice_maximum_fusion
  200.2 0.6 copy.32
  200.8 0.6 maximum_bitcast_fusion.4
  201.5 0.7 slice_bitcast_fusion
  202.2 0.7 slice.262
  202.9 0.6 dynamic-slice_bitcast_fusion
  (25 shorter events, 0.2 us)
Async XLA Ops:
  0.6 3.9 %copy-start.1 = (bf16[1,2,197,768]{3,1,2,0:T(2,128)(2,1)S(1)}, bf16[1,2,197,768]{3,1,2,0:T(2,128)(2,1)}, u32[]{:S(2)}) copy-start(bf16[1,2,197,768]{3,1,2,0:T(2,128)(2,1)} %param.10) | copy-start | bytes 1815556
  2.3 0.9 copy-start.2
  2.3 0.9 copy-start.3
  3.9 0.7 copy-start.8
  6.1 0.7 copy-start.4
  6.1 0.7 copy-start.5
  7.1 0.7 copy-start.7
  7.8 0.7 copy-start.6
  194.2 4.3 %copy-start = (f32[144,768]{1,0:T(8,128)S(1)}, f32[144,768]{1,0:T(8,128)}, u32[]{:S(2)}) copy-start(f32[144,768]{1,0:T(8,128)} %get-tuple-element.14) | copy-start | bytes 1327108

commit v3 on v2

--- a/solution.py
+++ b/solution.py
@@ -67,22 +67,30 @@
         order = ORDERS[self.third]
         axis = order[phase]
         me = self.coords[axis]
-        value = (me, me, lax.rem(me + 3, 4), lax.rem(me + 1, 4))[which]
-        ref = block_of(
-            self.buf, self.coords, self.kind, self.third, order[:phase], axis, value, (None, None, 0, 1)[which]
-        )
+        if phase == 0:
+            value, half, by = me, None, which + 1
+        else:
+            value = (me, me, lax.rem(me + 3, 4), lax.rem(me + 1, 4))[which]
+            half, by = (None, None, 0, 1)[which], (1, 3)[which % 2]
+        ref = block_of(self.buf, self.coords, self.kind, self.third, order[:phase], axis, value, half)
         return pltpu.make_async_remote_copy(
             src_ref=ref,
             dst_ref=ref,
             send_sem=self.send.at[self.sid, phase, which],
             recv_sem=self.recv.at[self.sid, phase, which],
-            device_id=device_at(moved(self.coords, axis, (1, 3)[which % 2])),
+            device_id=device_at(moved(self.coords, axis, by)),
             device_id_type=MESH,
         )
 
     def step(self, number):
         phase, stage = number // 3, number % 3
-        if stage == 0:
+        if phase == 0:
+            for which in range(3):
+                if stage == 0:
+                    self.copy(0, which).start()
+                elif stage == 2:
+                    self.copy(0, which).wait_recv()
+        elif stage == 0:
             self.copy(phase, 0).start()
             self.copy(phase, 1).start()
         elif stage == 1:
@@ -96,7 +104,7 @@
 
     def drain(self):
         for phase in range(3):
-            for which in range(4):
+            for which in range(4 if phase else 3):
                 self.copy(phase, which).wait_send()
 
 
@@ -112,23 +120,38 @@
         return block_of(self.buf, self.coords, self.kind, self.third, order[phase + 1 :], axis, value, half)
 
     def landing(self, phase, which):
+        if phase == 2:
+            return self.landings[4].at[self.sid, which]
         return self.landings[2 * phase + which // 2].at[self.sid, which % 2]
 
     def copy(self, phase, which):
         axis = ORDERS[self.third][::-1][phase]
-        by = (2, 2, 1, 3)[which]
+        if phase == 2:
+            block, to = self.block(2, which + 1, None), which + 1
+        else:
+            block, to = self.block(phase, (2, 2, 1, 3)[which], (0, 1, None, None)[which]), (1, 3)[which % 2]
         return pltpu.make_async_remote_copy(
-            src_ref=self.block(phase, by, (0, 1, None, None)[which]),
+            src_ref=block,
             dst_ref=self.landing(phase, which),
             send_sem=self.send.at[self.sid, phase, which],
             recv_sem=self.recv.at[self.sid, phase, which],
-            device_id=device_at(moved(self.coords, axis, (1, 3)[which % 2])),
+            device_id=device_at(moved(self.coords, axis, to)),
             device_id_type=MESH,
         )
 
     def step(self, number):
         phase, stage = number // 3, number % 3
-        if stage == 0:
+        if phase == 2:
+            if stage == 0:
+                for which in range(3):
+                    self.copy(2, which).start()
+            elif stage == 2:
+                total = self.block(2, 0, None)[...].astype(f32)
+                for which in range(3):
+                    self.copy(2, which).wait_recv()
+                    total = total + self.landing(2, which)[...].astype(f32)
+                self.out[pl.ds(self.kind * 48 + self.third * 16, 16), :] = total
+        elif stage == 0:
             self.copy(phase, 0).start()
             self.copy(phase, 1).start()
         elif stage == 1:
@@ -146,14 +169,11 @@
                 + self.landing(phase, 2)[...].astype(f32)
                 + self.landing(phase, 3)[...].astype(f32)
             )
-            if phase < 2:
-                mine[...] = total.astype(bf16)
-            else:
-                self.out[pl.ds(self.kind * 48 + self.third * 16, 16), :] = total
+            mine[...] = total.astype(bf16)
 
     def drain(self):
         for phase in range(3):
-            for which in range(4):
+            for which in range(4 if phase < 2 else 3):
                 self.copy(phase, which).wait_send()
 
 
@@ -194,8 +214,7 @@
     pltpu.VMEM((9, 2, 4, 4, 16, 768), bf16),
     pltpu.VMEM((9, 2, 2, 16, 768), bf16),
     pltpu.VMEM((9, 2, 4, 16, 768), bf16),
-    pltpu.VMEM((9, 2, 16, 384), bf16),
-    pltpu.VMEM((9, 2, 16, 768), bf16),
+    pltpu.VMEM((9, 3, 16, 768), bf16),
 ]
 
 
@@ -293,7 +312,7 @@
     lax.fori_loop(0, 4, head_group, 0)
 
 
-def forward_ffn(r):
+def forward_up(r):
     vec = r.vec
 
     def second_norm(rows, _):
@@ -312,6 +331,12 @@
             cdf = 0.5 * (1.0 + lax.erf(u * 0.7071067811865476))
             r.act[j, :, cols] = (u * cdf).astype(bf16)
             r.gp[j, :, cols] = (cdf + u * (jnp.exp(-0.5 * u * u) * 0.3989422804014327)).astype(bf16)
+        return 0
+    lax.fori_loop(0, 4, hidden, 0)
+
+
+def forward_down(r):
+    def hidden(j, _):
         r.acc[...] += nn(r.act[j], square(r.w, 2, j))
         return 0
     lax.fori_loop(0, 4, hidden, 0)
@@ -465,9 +490,9 @@
 def layer_kernel(w_hbm, rows_hbm, vec_hbm, end_hbm, grad_hbm, dvec_hbm, *scratch):
     r = types.SimpleNamespace(**dict(zip(NAMES, scratch)))
     rest = scratch[len(NAMES) :]
-    landings, out = rest[:6], r.h1
-    stages, sum_landings = rest[6:9], rest[9:12]
-    ag_send, ag_recv, rs_send, rs_recv, sum_send, sum_recv, link, local, ready = rest[12:]
+    landings, out = rest[:5], r.h1
+    stages, sum_landings = rest[5:8], rest[8:11]
+    ag_send, ag_recv, rs_send, rs_recv, sum_send, sum_recv, link, local, ready = rest[11:]
     coords = place()
     first = lax.axis_index("pipe") == 0
     second = lax.axis_index("pipe") == 1
@@ -561,8 +586,10 @@
         up.wait_recv()
 
     forward_attention(r)
-    each(late, 8)
-    forward_ffn(r)
+    each(gathers[3:6], 8)
+    forward_up(r)
+    each(gathers[6:], 8)
+    forward_down(r)
     r.dx[...] = r.acc[...].astype(bf16)
 
     @pl.when(first)
@@ -599,6 +626,7 @@
     sums[1].start(0)
     grads_up(r)
     each(su, 0)
+
     def during_attention(t):
         @pl.when(t == 3)
         def _():

time: 204 us -> 201 us (0.985)
  Pallas kernels: 183 us -> 180 us
    pallas_call x1, Pallas kernels: 183 us -> 180 us  [on_device(): pl.pallas_call(layer_kernel, out_shape=(jax.ShapeDtypeStruct((ROWS, 768),...]
where the time goes in v3:
time: 201 us; the launch traced here: 200 us
  Pallas kernels  180 us (90%)
  local copies, waits for them, and re-layouts  14.2 us (7%)
  other arithmetic  5.52 us (3%)
    pallas_call x1, Pallas kernels, on_device(): pl.pallas_call(layer_kernel, out_shape=(jax.ShapeDtypeStruct((ROWS, 768),...  180 us

profile of v3, /device:TPU:0, one launch (start us, length us, event | category | flops | bytes accessed | tf_op | source)
XLA Modules:
  0.0 200.4 jit_solution(13843803380240324015)
XLA Ops:
  0.6 0.0 copy-start.1
  0.7 0.9 slice_bitcast_fusion.2
  1.5 0.7 slice_bitcast_fusion.17
  2.3 0.0 copy-start.2
  2.3 0.0 copy-start.3
  2.3 0.1 concatenate.18
  2.4 0.7 copy-done.2
  3.2 0.0 copy-done.3
  3.2 0.7 pad_maximum_fusion.w_hbm
  3.9 0.0 copy-start.8
  3.9 0.7 copy-done.8
  4.6 0.0 copy-done.1
  4.6 0.6 broadcast_select_fusion.1
  5.2 0.1 copy.27
  5.2 0.9 pad.4.clone
  6.1 0.0 copy-start.4
  6.1 0.0 copy-start.5
  6.1 0.7 copy-done.4
  6.8 0.0 copy-done.5
  6.8 0.2 tile.32
  7.1 0.0 copy-start.7
  7.1 0.6 copy-done.7
  7.7 0.1 tile.35
  7.8 0.0 copy-start.6
  7.8 0.7 copy-done.6
  8.5 0.1 tile.39
  8.7 0.1 concatenate.22
  8.8 0.1 fusion.3
  8.9 1.3 concatenate.23.vec_hbm
  10.1 179.7 %shard_map.169 = (bf16[416,768]{1,0:T(8,128)(2,1)}, f32[144,768]{1,0:T(8,128)}, f32[16,768]{1,0:T(8,128)}) custom-call(bf16[3,48,768]{2,1,0:T(8,128)(2,1)} %pad_maximum_fusion.w_hbm, bf16[416,768]{1,0:T(8,128)(2,1)} %bitcast.129, bf16[16,768]{1,0:T(8,128)(2,1)} %concatenate.23.vec_hbm), custom_call_target="tpu_custom_call" | custom-call | tf_op jit(solution)/shard_map/pallas_call | solution.py:745
  189.9 1.1 slice.287
  191.0 0.0 copy-start
  191.0 1.5 fusion
  192.5 0.8 fusion.9
  193.3 0.6 maximum_bitcast_fusion.8
  193.9 0.8 dynamic-slice.3
  194.7 0.6 maximum_bitcast_fusion.5
  195.3 0.0 copy-done
  195.3 0.1 slice_bitcast_fusion.7
  195.4 0.7 maximum_bitcast_fusion
  196.1 0.8 constant_dynamic-slice_fusion
  197.0 0.1 dynamic-slice_maximum_fusion
  197.1 0.6 copy.32
  197.7 0.6 maximum_bitcast_fusion.4
  198.3 0.7 slice_bitcast_fusion
  199.0 0.7 slice.262
  199.8 0.6 dynamic-slice_bitcast_fusion
  (25 shorter events, 0.2 us)
Async XLA Ops:
  0.6 3.9 %copy-start.1 = (bf16[1,2,197,768]{3,1,2,0:T(2,128)(2,1)S(1)}, bf16[1,2,197,768]{3,1,2,0:T(2,128)(2,1)}, u32[]{:S(2)}) copy-start(bf16[1,2,197,768]{3,1,2,0:T(2,128)(2,1)} %param.10) | copy-start | bytes 1815556
  2.3 0.9 copy-start.2
  2.3 0.9 copy-start.3
  3.9 0.7 copy-start.8
  6.1 0.7 copy-start.4
  6.1 0.7 copy-start.5
  7.1 0.7 copy-start.7
  7.8 0.7 copy-start.6
  191.0 4.3 %copy-start = (f32[144,768]{1,0:T(8,128)S(1)}, f32[144,768]{1,0:T(8,128)}, u32[]{:S(2)}) copy-start(f32[144,768]{1,0:T(8,128)} %get-tuple-element.14) | copy-start | bytes 1327108

commit v4 on v3

--- a/solution.py
+++ b/solution.py
@@ -496,8 +496,6 @@
     coords = place()
     first = lax.axis_index("pipe") == 0
     second = lax.axis_index("pipe") == 1
-    enter(coords)
-
     own = [
         pltpu.make_async_copy(
             w_hbm.at[kind], r.w.at[(kind, *(coords[name] for name in LAYOUT[kind]))], local.at[kind]
@@ -509,18 +507,18 @@
     vec_in = pltpu.make_async_copy(vec_hbm, stages[0].at[0], local.at[3])
     vec_in.start()
 
+    to_x = pltpu.make_async_copy(rows_hbm, r.x, local.at[4])
+    to_gy = pltpu.make_async_copy(rows_hbm, r.gy, local.at[4])
+
     @pl.when(first)
     def _():
-        copy = pltpu.make_async_copy(rows_hbm, r.x, local.at[4])
-        copy.start()
-        copy.wait()
+        to_x.start()
 
     @pl.when(second)
     def _():
-        copy = pltpu.make_async_copy(rows_hbm, r.gy, local.at[4])
-        copy.start()
-        copy.wait()
-
+        to_gy.start()
+
+    enter(coords)
     for copy in own:
         copy.wait()
     vec_in.wait()
@@ -580,8 +578,13 @@
     )
     end = pltpu.make_async_copy(r.dx, end_hbm, local.at[5])
 
+    @pl.when(first)
+    def _():
+        to_x.wait()
+
     @pl.when(second)
     def _():
+        to_gy.wait()
         each(late, 7)
         up.wait_recv()
 

time: 201 us -> 200 us (level)
  no operation moved by 1% of the time
where the time goes in v4:
time: 200 us; the launch traced here: 199 us
  Pallas kernels  179 us (90%)
  local copies, waits for them, and re-layouts  14.2 us (7%)
  other arithmetic  5.52 us (3%)
    pallas_call x1, Pallas kernels, on_device(): pl.pallas_call(layer_kernel, out_shape=(jax.ShapeDtypeStruct((ROWS, 768),...  179 us

profile of v4, /device:TPU:0, one launch (start us, length us, event | category | flops | bytes accessed | tf_op | source)
XLA Modules:
  0.0 199.2 jit_solution(17187565591063071634)
XLA Ops:
  0.6 0.0 copy-start.1
  0.7 0.9 slice_bitcast_fusion.2
  1.5 0.7 slice_bitcast_fusion.17
  2.3 0.0 copy-start.2
  2.3 0.0 copy-start.3
  2.3 0.1 concatenate.18
  2.4 0.7 copy-done.2
  3.2 0.0 copy-done.3
  3.2 0.7 pad_maximum_fusion.w_hbm
  3.9 0.0 copy-start.8
  3.9 0.7 copy-done.8
  4.6 0.0 copy-done.1
  4.6 0.6 broadcast_select_fusion.1
  5.2 0.1 copy.27
  5.2 0.9 pad.4.clone
  6.1 0.0 copy-start.4
  6.1 0.0 copy-start.5
  6.1 0.7 copy-done.4
  6.8 0.0 copy-done.5
  6.8 0.2 tile.32
  7.1 0.0 copy-start.7
  7.1 0.6 copy-done.7
  7.7 0.1 tile.35
  7.8 0.0 copy-start.6
  7.8 0.7 copy-done.6
  8.5 0.1 tile.39
  8.7 0.1 concatenate.22
  8.8 0.1 fusion.3
  8.9 1.3 concatenate.23.vec_hbm
  10.1 178.5 %shard_map.169 = (bf16[416,768]{1,0:T(8,128)(2,1)}, f32[144,768]{1,0:T(8,128)}, f32[16,768]{1,0:T(8,128)}) custom-call(bf16[3,48,768]{2,1,0:T(8,128)(2,1)} %pad_maximum_fusion.w_hbm, bf16[416,768]{1,0:T(8,128)(2,1)} %bitcast.129, bf16[16,768]{1,0:T(8,128)(2,1)} %concatenate.23.vec_hbm), custom_call_target="tpu_custom_call" | custom-call | tf_op jit(solution)/shard_map/pallas_call | solution.py:748
  188.7 1.1 slice.287
  189.8 0.0 copy-start
  189.8 1.5 fusion
  191.3 0.8 fusion.9
  192.1 0.6 maximum_bitcast_fusion.8
  192.7 0.8 dynamic-slice.3
  193.5 0.6 maximum_bitcast_fusion.5
  194.1 0.0 copy-done
  194.1 0.1 slice_bitcast_fusion.7
  194.2 0.7 maximum_bitcast_fusion
  194.9 0.8 constant_dynamic-slice_fusion
  195.8 0.1 dynamic-slice_maximum_fusion
  195.9 0.6 copy.32
  196.5 0.6 maximum_bitcast_fusion.4
  197.1 0.7 slice_bitcast_fusion
  197.8 0.7 slice.262
  198.6 0.6 dynamic-slice_bitcast_fusion
  (25 shorter events, 0.2 us)
Async XLA Ops:
  0.6 3.9 %copy-start.1 = (bf16[1,2,197,768]{3,1,2,0:T(2,128)(2,1)S(1)}, bf16[1,2,197,768]{3,1,2,0:T(2,128)(2,1)}, u32[]{:S(2)}) copy-start(bf16[1,2,197,768]{3,1,2,0:T(2,128)(2,1)} %param.10) | copy-start | bytes 1815556
  2.3 0.9 copy-start.2
  2.3 0.9 copy-start.3
  3.9 0.7 copy-start.8
  6.1 0.7 copy-start.4
  6.1 0.7 copy-start.5
  7.1 0.7 copy-start.7
  7.8 0.7 copy-start.6
  189.8 4.3 %copy-start = (f32[144,768]{1,0:T(8,128)S(1)}, f32[144,768]{1,0:T(8,128)}, u32[]{:S(2)}) copy-start(f32[144,768]{1,0:T(8,128)} %get-tuple-element.14) | copy-start | bytes 1327108

commit v5 on v4

--- a/solution.py
+++ b/solution.py
@@ -416,17 +416,17 @@
                 dv = nn(p, d_full)
                 dp = nt(v, d_masked)
                 ds = (pf * (dp - jnp.sum(dp * pf, 0, keepdims=True))).astype(bf16)
-                return nn(kt, ds), nn(ds, q) * 0.125, dv
+                return nn(kt, ds), nn(ds, q), dv
             tkt = tk.T
             dq0, dk0, dv0 = head(0, d5, jnp.where(low, d5, zero), tv, tq, tkt[0:64])
             dq1, dk1, dv1 = head(1, d5, jnp.where(low, zero, d5), tv, tq, tkt[64:128])
             dq2, dk2, dv2 = head(2, d4, jnp.where(low, zero, d4), t3, t3, t4.T[0:64])
             r.q[t, rows, 0:128] = (jnp.concatenate([dq0, dq1], 0) * 0.125).astype(bf16).T
-            r.q[t, rows, 128:256] = jnp.where(low, dk0, dk1).astype(bf16)
+            r.q[t, rows, 128:256] = (jnp.where(low, dk0, dk1) * 0.125).astype(bf16)
             r.q[t, rows, 256:384] = jnp.where(low, dv0, dv1).astype(bf16)
             dq2 = jnp.concatenate([(dq2 * 0.125).astype(bf16), jnp.zeros((64, IMG), bf16)], 0).T
             r.q[t, rows, 384:512] = jnp.where(low, dq2, dv2.astype(bf16))
-            r.q[t, rows, 512:640] = jnp.where(low, dk2, 0.0).astype(bf16)
+            r.q[t, rows, 512:640] = jnp.where(low, dk2 * 0.125, 0.0).astype(bf16)
         image(0)
         image(1)
         dvec[pl.ds(10 + t, 1), 0:640] = jnp.sum(r.q[t].astype(f32), 0, keepdims=True)
@@ -631,12 +631,15 @@
     each(su, 0)
 
     def during_attention(t):
+        @pl.when(t == 1)
+        def _():
+            each(su, 1)
+
         @pl.when(t == 3)
         def _():
             sums[1].finish(0)
             sums[1].start(1)
             each(sd, 2, 3)
-            each(su, 1)
 
     backward_attention(r, during_attention)
 

time: 200 us -> 199 us (level)
  no operation moved by 1% of the time
where the time goes in v5:
time: 199 us; the launch traced here: 198 us
  Pallas kernels  178 us (89%)
  local copies, waits for them, and re-layouts  14.2 us (7%)
  other arithmetic  5.52 us (3%)
    pallas_call x1, Pallas kernels, on_device(): pl.pallas_call(layer_kernel, out_shape=(jax.ShapeDtypeStruct((ROWS, 768),...  178 us

profile of v5, /device:TPU:0, one launch (start us, length us, event | category | flops | bytes accessed | tf_op | source)
XLA Modules:
  0.0 198.4 jit_solution(15802471611024580068)
XLA Ops:
  0.6 0.0 copy-start.1
  0.7 0.9 slice_bitcast_fusion.2
  1.5 0.7 slice_bitcast_fusion.17
  2.3 0.0 copy-start.2
  2.3 0.0 copy-start.3
  2.3 0.1 concatenate.18
  2.4 0.7 copy-done.2
  3.2 0.0 copy-done.3
  3.2 0.7 pad_maximum_fusion.w_hbm
  3.9 0.0 copy-start.8
  3.9 0.7 copy-done.8
  4.6 0.0 copy-done.1
  4.6 0.6 broadcast_select_fusion.1
  5.2 0.1 copy.27
  5.2 0.9 pad.4.clone
  6.1 0.0 copy-start.4
  6.1 0.0 copy-start.5
  6.1 0.7 copy-done.4
  6.8 0.0 copy-done.5
  6.8 0.2 tile.32
  7.1 0.0 copy-start.7
  7.1 0.6 copy-done.7
  7.7 0.1 tile.35
  7.8 0.0 copy-start.6
  7.8 0.7 copy-done.6
  8.5 0.1 tile.39
  8.7 0.1 concatenate.22
  8.8 0.1 fusion.3
  8.9 1.3 concatenate.23.vec_hbm
  10.1 177.8 %shard_map.169 = (bf16[416,768]{1,0:T(8,128)(2,1)}, f32[144,768]{1,0:T(8,128)}, f32[16,768]{1,0:T(8,128)}) custom-call(bf16[3,48,768]{2,1,0:T(8,128)(2,1)} %pad_maximum_fusion.w_hbm, bf16[416,768]{1,0:T(8,128)(2,1)} %bitcast.129, bf16[16,768]{1,0:T(8,128)(2,1)} %concatenate.23.vec_hbm), custom_call_target="tpu_custom_call" | custom-call | tf_op jit(solution)/shard_map/pallas_call | solution.py:751
  188.0 1.1 slice.287
  189.1 0.0 copy-start
  189.1 1.5 fusion
  190.6 0.8 fusion.9
  191.4 0.6 maximum_bitcast_fusion.8
  192.0 0.8 dynamic-slice.3
  192.8 0.6 maximum_bitcast_fusion.5
  193.3 0.0 copy-done
  193.3 0.1 slice_bitcast_fusion.7
  193.5 0.7 maximum_bitcast_fusion
  194.2 0.8 constant_dynamic-slice_fusion
  195.1 0.1 dynamic-slice_maximum_fusion
  195.1 0.6 copy.32
  195.7 0.6 maximum_bitcast_fusion.4
  196.4 0.7 slice_bitcast_fusion
  197.1 0.7 slice.262
  197.9 0.6 dynamic-slice_bitcast_fusion
  (25 shorter events, 0.2 us)
Async XLA Ops:
  0.6 3.9 %copy-start.1 = (bf16[1,2,197,768]{3,1,2,0:T(2,128)(2,1)S(1)}, bf16[1,2,197,768]{3,1,2,0:T(2,128)(2,1)}, u32[]{:S(2)}) copy-start(bf16[1,2,197,768]{3,1,2,0:T(2,128)(2,1)} %param.10) | copy-start | bytes 1815556
  2.3 0.9 copy-start.2
  2.3 0.9 copy-start.3
  3.9 0.7 copy-start.8
  6.1 0.7 copy-start.4
  6.1 0.7 copy-start.5
  7.1 0.7 copy-start.7
  7.8 0.7 copy-start.6
  189.1 4.3 %copy-start = (f32[144,768]{1,0:T(8,128)S(1)}, f32[144,768]{1,0:T(8,128)}, u32[]{:S(2)}) copy-start(f32[144,768]{1,0:T(8,128)} %get-tuple-element.14) | copy-start | bytes 1327108
